TPU v7x, 512 devices: a whole 4x4x16 slice. The times are simulated.
512 devices in a mesh: sample: 16 (over x, y_lo, core), space: 32 (over y_hi, z).
Axes of the slice: x: 4, y: 4 (y_hi: 2, y_lo: 2; y = y_hi * 2 + y_lo), z: 16, core: 2. Of those that a mesh axis runs over, the one named last changes fastest.
Arguments:
- fields: bfloat16 [16, 4, 64, 24, 256], P('sample', None, 'space'), may hold values from -6 to 6
- cotangent: bfloat16 [16, 4, 64, 24, 256], P('sample', None, 'space'), may hold values from -6 to 6
- w_in: bfloat16 [27, 32, 4], replicated, may hold values from -0.625 to 0.625
- w_down: bfloat16 [8, 64, 32], replicated, may hold values from -0.375 to 0.375
- w_coarse: bfloat16 [27, 64, 64], replicated, may hold values from -0.15625 to 0.15625
- w_up: bfloat16 [8, 32, 64], replicated, may hold values from -0.75 to 0.75
- w_out: bfloat16 [4, 32], replicated, may hold values from -1 to 1
Outputs:
- prediction: bfloat16 [16, 4, 64, 24, 256], P('sample', None, 'space')
- grad_in: float32 [27, 32, 4], replicated
- grad_down: float32 [8, 64, 32], replicated
- grad_coarse: float32 [27, 64, 64], replicated
- grad_up: float32 [8, 32, 64], replicated
- grad_out: float32 [4, 32], replicated
All inputs are finite; a program needn't handle non-finite values.
Results may differ from a plain program's by a relative error of at most 0.018.
Values may be sent and summed in bfloat16 or wider, within the bound.
A program may use at most 64 MiB of HBM per device.

v0:
```python
import jax
import jax.numpy as jnp
from jax import lax
from jax.sharding import PartitionSpec as P


def with_halo(cells, sides, width):
    for axis, dim in sides:
        count = lax.axis_size(axis)
        ends = count - 1
        head = lax.slice_in_dim(cells, 0, width, axis=dim)
        tail = lax.slice_in_dim(cells, cells.shape[dim] - width, cells.shape[dim], axis=dim)
        cells = jnp.concatenate(
            [
                lax.ppermute(tail, axis, [(i, (i + 1) % count) for i in range(ends)]),
                cells,
                lax.ppermute(head, axis, [((i + 1) % count, i) for i in range(ends)]),
            ],
            axis=dim,
        )
    return cells


def pad_sides(volume):
    return jnp.pad(volume, ((0, 0), (0, 0), (1, 1), (1, 1)))


def all_taps(padded, dims):
    depth, height, width = dims
    windows = []
    for first in range(3):
        for second in range(3):
            for third in range(3):
                windows.append(
                    padded[
                        :, first : first + depth, second : second + height, third : third + width
                    ]
                )
    return jnp.stack(windows)


def row_taps(padded, dims, first, second):
    depth, height, width = dims
    return jnp.stack(
        [
            padded[:, first : first + depth, second : second + height, third : third + width]
            for third in range(3)
        ]
    )


def conv_whole(padded, weights, dims):
    return jnp.einsum(
        "toc,tcxyz->oxyz", weights, all_taps(padded, dims), preferred_element_type=jnp.float32
    )


def weight_grad_whole(gradient, padded, dims):
    return jnp.einsum(
        "oxyz,tcxyz->toc", gradient, all_taps(padded, dims), preferred_element_type=jnp.float32
    )


def conv_rows(padded, weights, dims):
    depth, height, width = dims
    summed = jnp.zeros((weights.shape[1], depth, height, width), jnp.float32)
    for first in range(3):
        for second in range(3):
            start = 9 * first + 3 * second
            window = row_taps(padded, dims, first, second)
            summed = summed + jnp.einsum(
                "toc,tcxyz->oxyz",
                weights[start : start + 3],
                window,
                preferred_element_type=jnp.float32,
            )
    return summed


def weight_grad_rows(gradient, padded, dims):
    pieces = []
    for first in range(3):
        for second in range(3):
            window = row_taps(padded, dims, first, second)
            pieces.append(
                jnp.einsum("oxyz,tcxyz->toc", gradient, window, preferred_element_type=jnp.float32)
            )
    return jnp.concatenate(pieces, axis=0)


def data_grad_rows(grad_padded, weights, dims):
    depth, height, width = dims
    summed = jnp.zeros((weights.shape[2], depth, height, width), jnp.float32)
    for first in range(3):
        for second in range(3):
            start = 9 * first + 3 * second
            window = jnp.stack(
                [
                    grad_padded[
                        :,
                        2 - first : 2 - first + depth,
                        2 - second : 2 - second + height,
                        2 - third : 2 - third + width,
                    ]
                    for third in range(3)
                ]
            )
            summed = summed + jnp.einsum(
                "toc,toxyz->cxyz",
                weights[start : start + 3],
                window,
                preferred_element_type=jnp.float32,
            )
    return summed


def silu_slope(value):
    sigma = jax.nn.sigmoid(value)
    return sigma * (1.0 + value * (1.0 - sigma))


def reduce_term(term):
    return lax.psum(term, ("sample", "space"))


def settle(term):
    return reduce_term(term)


def shards(fields, cotangent, w_in, w_down, w_coarse, w_up, w_out):
    volume = fields[0]
    cot_volume = cotangent[0]
    depth, height, width = (volume.shape[1], volume.shape[2], volume.shape[3])
    chan_fine = w_in.shape[1]
    chan_coarse = w_coarse.shape[1]
    fine_dims = (depth, height, width)
    coarse_dims = (depth // 2, height // 2, width // 2)
    down_five = w_down.reshape(2, 2, 2, chan_coarse, chan_fine)
    up_five = w_up.reshape(2, 2, 2, chan_fine, chan_coarse)
    field_pad = pad_sides(with_halo(volume, (("space", 1),), 1))
    pre_fine = conv_whole(field_pad, w_in, fine_dims)
    act_fine = jax.nn.silu(pre_fine).astype(jnp.bfloat16)
    act_six = act_fine.reshape(chan_fine, coarse_dims[0], 2, coarse_dims[1], 2, coarse_dims[2], 2)
    reduced = jnp.einsum(
        "ijkoc,cxiyjzk->oxyz", down_five, act_six, preferred_element_type=jnp.float32
    ).astype(jnp.bfloat16)
    reduced_pad = pad_sides(with_halo(reduced, (("space", 1),), 1))
    pre_coarse = conv_rows(reduced_pad, w_coarse, coarse_dims)
    act_coarse = jax.nn.silu(pre_coarse).astype(jnp.bfloat16)
    upward = jnp.einsum(
        "ijkoc,cxyz->oxiyjzk", up_five, act_coarse, preferred_element_type=jnp.float32
    ).reshape(chan_fine, depth, height, width)
    merged = (act_fine.astype(jnp.float32) + upward).astype(jnp.bfloat16)
    prediction = jnp.einsum(
        "fc,cxyz->fxyz", w_out, merged, preferred_element_type=jnp.float32
    ).astype(jnp.bfloat16)
    grad_out = settle(
        jnp.einsum("fxyz,cxyz->fc", cot_volume, merged, preferred_element_type=jnp.float32)
    )
    back_merged = jnp.einsum(
        "fc,fxyz->cxyz", w_out, cot_volume, preferred_element_type=jnp.float32
    ).astype(jnp.bfloat16)
    back_six = back_merged.reshape(
        chan_fine, coarse_dims[0], 2, coarse_dims[1], 2, coarse_dims[2], 2
    )
    grad_up = settle(
        jnp.einsum(
            "oxiyjzk,cxyz->ijkoc", back_six, act_coarse, preferred_element_type=jnp.float32
        ).reshape(8, chan_fine, chan_coarse)
    )
    coarse_term = jnp.einsum(
        "ijkoc,oxiyjzk->cxyz", up_five, back_six, preferred_element_type=jnp.float32
    )
    back_coarse = (coarse_term * silu_slope(pre_coarse)).astype(jnp.bfloat16)
    back_pad = pad_sides(with_halo(back_coarse, (("space", 1),), 1))
    grad_coarse = settle(weight_grad_rows(back_coarse, reduced_pad, coarse_dims))
    back_reduced = data_grad_rows(back_pad, w_coarse, coarse_dims).astype(jnp.bfloat16)
    grad_down = settle(
        jnp.einsum(
            "oxyz,cxiyjzk->ijkoc", back_reduced, act_six, preferred_element_type=jnp.float32
        ).reshape(8, chan_coarse, chan_fine)
    )
    spread = jnp.einsum(
        "ijkoc,oxyz->cxiyjzk", down_five, back_reduced, preferred_element_type=jnp.float32
    ).reshape(chan_fine, depth, height, width)
    back_fine = ((back_merged.astype(jnp.float32) + spread) * silu_slope(pre_fine)).astype(
        jnp.bfloat16
    )
    grad_in = settle(weight_grad_whole(back_fine, field_pad, fine_dims))
    return (prediction[None], grad_in, grad_down, grad_coarse, grad_up, grad_out)


def solution(mesh):
    placed = (
        P("sample", None, "space", None, None),
        P("sample", None, "space", None, None),
        P(),
        P(),
        P(),
        P(),
        P(),
    )
    return jax.shard_map(
        shards,
        mesh=mesh,
        in_specs=placed,
        out_specs=(P("sample", None, "space", None, None), P(), P(), P(), P(), P()),
        check_vma=False,
    )
```

profile of v0, /device:TPU:1, one launch (start us, length us, event | category | flops | bytes accessed | tf_op | source)
XLA Modules:
  0.0 613.5 jit_solution(3727413247040507526)
XLA Ops:
  8.1 4.4 collective-permute-start
  12.4 1.3 collective-permute-start.1
  14.8 2.7 collective-permute-done.1
  17.5 1.2 select_maximum_fusion.4
  30.6 17.3 %stack.388 = bf16[27,4,2,24,256]{4,0,1,3,2:T(8,128)(2,1)} concatenate(bf16[1,4,2,24,256]{4,0,1,3,2:T(2,128)(2,1)S(1)} %copy.1724, bf16[1,4,2,24,256]{4,0,1,3,2:T(2,128)(2,1)S(1)} %copy.1725, bf16[1,4,2,24,256]{4,0,1,3,2:T(2,128)(2,1)S(1)} %copy.1726, bf16[1,4,2,24,256]{4,0,1,3,2:T(2,128)(2,1)S(1)} %copy.1727, bf16[1,4,2,24,256]{4,0,1,3,2:T(2,128)(2,1)S(1)} %copy.1728, ...), dimensions={0} | concatenate | bytes 5308416 | tf_op jit(solution)/shard_map/stack | solution.py:39
  47.9 3.7 fusion.14
  51.6 2.7 copy.1752
  54.4 3.0 fusion.50
  57.4 1.3 collective-permute-start.3
  58.7 4.7 collective-permute-start.2
  63.8 2.7 copy.1757
  72.5 1.6 fusion
  75.3 1.4 collective-permute-start.5
  76.7 5.3 collective-permute-start.4
  90.6 6.4 %copy.1754 = f32[32,1,2,12,2,128,2]{0,6,5,4,3,2,1:T(2,128)} copy(f32[32,1,2,12,2,128,2]{5,0,6,4,2,3,1:T(8,128)S(1)} %convolution_bitcast_fusion.1) | data formatting | bytes 3145728 | tf_op jit(solution)/shard_map/ijkoc,cxyz->oxiyjzk/transpose | solution.py:150
  96.9 4.3 copy.1755
  107.1 1.4 copy-done.2
  108.5 1.6 fusion.2
  110.5 6.4 %copy.1768 = f32[32,1,2,12,2,128,2]{0,6,5,4,3,2,1:T(2,128)} copy(f32[32,1,2,12,2,128,2]{5,0,6,4,2,3,1:T(8,128)S(1)} %convolution_bitcast_fusion) | data formatting | bytes 3145728 | tf_op jit(solution)/shard_map/ijkoc,oxyz->cxiyjzk/transpose | solution.py:183
  116.9 5.7 copy.1769
  122.7 3.1 convolution_bitcast_fusion.29
  125.7 118.9 %all-reduce.3 = (f32[27,32,4]{1,0,2:T(8,128)S(1)}, f32[4,32]{1,0:T(4,128)}) all-reduce(f32[27,32,4]{1,0,2:T(8,128)S(1)} %convolution_bitcast_fusion.29, f32[4,32]{1,0:T(4,128)S(1)} %convolution_bitcast_fusion.30), channel_id=1, replica_groups=mesh['sample'=16,'space'=32] {'sample','space'}, use_global_device_ids=true, to_apply=%region_0.1 | all-reduce | flops 3584 | bytes 28672 | tf_op jit(solution)/shard_map/psum | solution.py:123
  245.3 357.7 %all-reduce.7.cloned.1.call-done = (f32[8,64,32]{1,2,0:T(8,128)}, f32[27,64,64]{1,2,0:T(8,128)}, f32[8,32,64]{2,1,0:T(8,128)}) async-done(((f32[8,64,32]{1,2,0:T(8,128)}, f32[27,64,64]{1,2,0:T(8,128)}, f32[8,32,64]{2,1,0:T(8,128)}), (f32[8,64,32]{1,2,0:T(8,128)}, f32[27,64,64]{1,2,0:T(8,128)}, f32[8,32,64]{2,1,0:T(8,128)})) %all-reduce.7.cloned.1.call-update) | async-done | bytes 573456 | tf_op jit(solution)/shard_map/psum | solution.py:123
  602.9 2.4 copy.1775
  (112 shorter events, 37.7 us)
Async XLA Ops:
  7.2 56.2 %copy-start = (bf16[1,4,2,24,256]{4,3,2,1,0:T(8,128)(2,1)S(1)}, bf16[1,4,2,24,256]{4,3,2,1,0:T(8,128)(2,1)}, u32[]{:S(2)}) copy-start(bf16[1,4,2,24,256]{4,3,2,1,0:T(8,128)(2,1)} %param.8) | copy-start | bytes 294916
  7.2 595.8 %all-reduce.7.cloned.1.call-start = ((), (), s32[]{:S(2)}) async-start(), calls=%async_computation | async-start | bytes 2293760 | tf_op jit(solution)/shard_map/psum | solution.py:123
  8.1 6.7 %collective-permute-start = (bf16[4,1,24,256]{3,2,1,0:T(8,128)(2,1)S(1)}, bf16[4,1,24,256]{3,2,1,0:T(8,128)(2,1)S(1)}, u32[]{:S(2)}, u32[]{:S(2)}) collective-permute-start(bf16[4,1,24,256]{3,2,1,0:T(8,128)(2,1)S(1)} %get-tuple-element.247), channel_id=1, source_target_pairs={{0,1},{1,2},{2,3},{3,4},{4,5},{5,6},{6,7},{7,8},{8,9},{9,10},{10,1... | collective-permute-start | bytes 147464 | tf_op jit(solution)/shard_map/ppermute | solution.py:15
  12.4 5.0 collective-permute-start.1
  18.8 0.9 copy-start.5
  30.6 17.3 %copy-start.15 = (bf16[27,32,4]{1,2,0:T(4,128)(2,1)S(1)}, bf16[27,32,4]{1,2,0:T(4,128)(2,1)}, u32[]{:S(2)}) copy-start(bf16[27,32,4]{1,2,0:T(4,128)(2,1)} %param.9) | copy-start | bytes 20740
  51.6 2.8 copy-start.11
  54.4 9.0 %copy-start.14 = (bf16[4,32]{1,0:T(4,128)(2,1)S(1)}, bf16[4,32]{1,0:T(4,128)(2,1)}, u32[]{:S(2)}) copy-start(bf16[4,32]{1,0:T(4,128)(2,1)} %param.13) | copy-start | bytes 772
  57.4 9.1 %collective-permute-start.3 = (bf16[64,1,12,128]{3,0,2,1:T(8,128)(2,1)S(1)}, bf16[64,1,12,128]{3,0,2,1:T(8,128)(2,1)S(1)}, u32[]{:S(2)}, u32[]{:S(2)}) collective-permute-start(bf16[64,1,12,128]{3,0,2,1:T(8,128)(2,1)S(1)} %bitcast.619), channel_id=1, source_target_pairs={{1,0},{2,1},{3,2},{4,3},{5,4},{6,5},{7,6},{8,7},{9,8},{10,9},{11,1... | collective-permute-start | bytes 589832 | tf_op jit(solution)/shard_map/ppermute | solution.py:17
  58.7 7.8 %collective-permute-start.2 = (bf16[64,1,12,128]{3,0,2,1:T(8,128)(2,1)S(1)}, bf16[64,1,12,128]{3,0,2,1:T(8,128)(2,1)S(1)}, u32[]{:S(2)}, u32[]{:S(2)}) collective-permute-start(bf16[64,1,12,128]{3,0,2,1:T(8,128)(2,1)S(1)} %bitcast.620), channel_id=1, source_target_pairs={{0,1},{1,2},{2,3},{3,4},{4,5},{5,6},{6,7},{7,8},{8,9},{9,10},{10,1... | collective-permute-start | bytes 589832 | tf_op jit(solution)/shard_map/ppermute | solution.py:15
  63.8 2.7 copy-start.4
  66.5 1.9 copy-start.6
  67.4 1.0 copy-start.12
  70.6 0.8 copy-start.10
  70.6 1.9 copy-start.3
  75.3 7.7 %copy-start.7 = (bf16[64,1,12,128]{3,0,2,1:T(8,128)(2,1)S(1)}, bf16[64,1,12,128]{3,0,2,1:T(8,128)(2,1)}, u32[]{:S(2)}) copy-start(bf16[64,1,12,128]{3,0,2,1:T(8,128)(2,1)} %copy-done.6) | copy-start | bytes 589828
  75.3 27.3 %collective-permute-start.5 = (bf16[64,1,12,128]{3,0,2,1:T(8,128)(2,1)S(1)}, bf16[64,1,12,128]{3,0,2,1:T(8,128)(2,1)S(1)}, u32[]{:S(2)}, u32[]{:S(2)}) collective-permute-start(bf16[64,1,12,128]{3,0,2,1:T(8,128)(2,1)S(1)} %bitcast.612), channel_id=1, source_target_pairs={{1,0},{2,1},{3,2},{4,3},{5,4},{6,5},{7,6},{8,7},{9,8},{10,9},{11,1... | collective-permute-start | bytes 589832 | tf_op jit(solution)/shard_map/ppermute | solution.py:17
  76.7 25.8 %collective-permute-start.4 = (bf16[64,1,12,128]{3,0,2,1:T(8,128)(2,1)S(1)}, bf16[64,1,12,128]{3,0,2,1:T(8,128)(2,1)S(1)}, u32[]{:S(2)}, u32[]{:S(2)}) collective-permute-start(bf16[64,1,12,128]{3,0,2,1:T(8,128)(2,1)S(1)} %bitcast.613), channel_id=1, source_target_pairs={{0,1},{1,2},{2,3},{3,4},{4,5},{5,6},{6,7},{7,8},{8,9},{9,10},{10,1... | collective-permute-start | bytes 589832 | tf_op jit(solution)/shard_map/ppermute | solution.py:15
  103.4 1.0 copy-start.13
  106.6 1.9 copy-start.2
  116.9 5.7 copy-start.1
  602.9 2.4 copy-start.9
  602.9 3.1 copy-start.8
Sparse Core Ops, SparseCore 0:
  122.8 480.1 all-reduce.6
where the time goes:
time: 616 us; the launch traced here: 614 us
  waiting for transfers between devices  360 us (58%)
  blocking collectives  119 us (19%)
  local copies, waits for them, and re-layouts  69.6 us (11%)
  matrix products  29.4 us (5%)
  starting transfers between devices  18.4 us (3%)
  between operations  14.6 us (2%)
    psum x1, waiting for transfers between devices, reduce_term(): return lax.psum(term, ('sample', 'space'))  358 us
    psum x1, blocking collectives, reduce_term(): return lax.psum(term, ('sample', 'space'))  119 us
    another operation x29, local copies, waits for them, and re-layouts, all_taps(): return jnp.stack(windows)  28.8 us
    ppermute x3, starting transfers between devices, with_halo(): lax.ppermute(tail, axis, [(i, (i + 1) % count) for i in range(ends)])  14.3 us
  transfers between devices with their start and end apart: 7, of which 2 were waited for; matrix products, arithmetic and copies ran while one was open for 5% of the time, Pallas kernels for 0%

commit v1 on v0

v1 whole, which is shorter than its diff:
```python
import functools

import jax
import jax.numpy as jnp
import numpy as np
from jax import lax
from jax.experimental import pallas as pl
from jax.experimental.pallas import tpu as pltpu
from jax.sharding import PartitionSpec as P

MESH = pl.DeviceIdType.MESH
BF = jnp.bfloat16
F32 = jnp.float32
LANES = 128
CHUNK = 256
HIGH = 2


def dot(a, b):
    return lax.dot_general(a, b, (((1,), (0,)), ((), ())), preferred_element_type=F32)


def dot_nt(a, b):
    return lax.dot_general(a, b, (((1,), (1,)), ((), ())), preferred_element_type=F32)


def one_hots(ny, nz, nf):
    wide = nz // 2
    rows = (ny + 2) * 4 * nf
    perm = np.zeros((rows, 4 * nf * ny), np.float32)
    own = 2 * nf * ny
    for y in range(ny):
        for f in range(nf):
            for dx in range(4):
                if dx == 0:
                    source = own + f * ny + y
                elif dx == 3:
                    source = own + nf * ny + f * ny + y
                else:
                    source = (f * 2 + dx - 1) * ny + y
                perm[(y + 1) * 4 * nf + dx * nf + f, source] = 1
    perm2 = np.zeros((2 * nf * ny, 2 * nf * ny), np.float32)
    for y in range(ny):
        for x in range(2):
            for f in range(nf):
                perm2[y * 2 * nf + x * nf + f, (f * 2 + x) * ny + y] = 1
    split = np.zeros((nz, 4 * wide), np.float32)
    for d in range(4):
        for z in range(wide):
            if 0 <= 2 * z + d - 1 < nz:
                split[2 * z + d - 1, d * wide + z] = 1
    join = split[:, wide : 3 * wide].T.copy()
    fold = np.zeros((128, 8 * 64 * nf), np.float32)
    for m in range(8):
        mz, my, mx = m // 4, m // 2 % 2, m % 2
        for k in range(27):
            dx, dy, dz = k // 9 + mx, k // 3 % 3 + my, k % 3 + mz
            for c in range(nf):
                fold[k * nf + c, m * 64 * nf + (dy * 4 + dz) * 4 * nf + dx * nf + c] = 1
    return [jnp.asarray(v, BF) for v in (perm, perm2, perm2.T.copy(), split, join, fold)]


def part_of(m):
    return 4 * (m % 2) + 2 * (m // 2 % 2) + m // 4


def body(
    ns, nspace,
    fields, cot, w_in, w_dn, w_co, w_up, w_out, perm, perm2, perm2t, split, join, fold,
    pred, g_in, g_dn, g_co, g_up, g_out,
    f_land, ff, tt, patches, win, win_t, wdt, wd, wu, wut, bd, bdt, wf, wb, wa,
    act, slope, cots, cot_t, bm, term, red, r_land, bc, b_land, rolled, act_c, pred_t, bf,
    red_out, bc_out,
    gi_wide, gc, e_send, e_recv, l_send, l_recv, late, z_send, z_recv, z_out, z_all,
    e_out, e_all, l_out, l_all, full,
    halo_ss, halo_rs, e_ss, e_rs, l_ss, l_rs, z_ss, z_rs, y_ss, y_rs, a_ss, a_rs, b_ss, b_rs,
):
    nzg = nspace // HIGH
    nxy = ns * HIGH
    s = lax.axis_index("sample")
    sp = lax.axis_index("space")
    high, zi = sp // nzg, lax.rem(sp, nzg)
    me = high * ns + s
    left = lax.rem(sp + nspace - 1, nspace)
    right = lax.rem(sp + 1, nspace)
    has_left = jnp.where(sp > 0, 1.0, 0.0).astype(F32)
    has_right = jnp.where(sp < nspace - 1, 1.0, 0.0).astype(F32)

    def plane_peer(i):
        peer = lax.rem(me + i, nxy)
        return peer, (lax.rem(peer, ns), (peer // ns) * nzg + zi)

    def z_peer(i):
        peer = lax.rem(zi + i, nzg)
        return peer, (s, high * nzg + peer)

    barrier = pltpu.get_barrier_semaphore()

    def greet(device):
        pl.semaphore_signal(barrier, inc=1, device_id=device, device_id_type=MESH)

    greet((s, left))
    greet((s, right))

    def greet_plane(i, carry):
        greet(plane_peer(i)[1])
        return carry

    def greet_z(i, carry):
        greet(z_peer(i)[1])
        return carry

    lax.fori_loop(1, nxy, greet_plane, 0)
    lax.fori_loop(1, nzg, greet_z, 0)
    pl.semaphore_wait(barrier, 2 + nxy - 1 + nzg - 1)

    def halo(step, to_left, to_right, land):
        copies = [
            pltpu.make_async_remote_copy(
                src_ref=to_right, dst_ref=land.at[0], send_sem=halo_ss.at[2 * step],
                recv_sem=halo_rs.at[2 * step], device_id=(s, right), device_id_type=MESH,
            ),
            pltpu.make_async_remote_copy(
                src_ref=to_left, dst_ref=land.at[1], send_sem=halo_ss.at[2 * step + 1],
                recv_sem=halo_rs.at[2 * step + 1], device_id=(s, left), device_id_type=MESH,
            ),
        ]
        for copy in copies:
            copy.start()
        return copies

    def finish(copies):
        for copy in copies:
            copy.wait()

    nf, ny, nz = fields.shape[1], fields.shape[3], fields.shape[4]
    c1, c2 = w_up.shape[1], w_up.shape[2]
    yc = ny // 2
    cells = yc * LANES
    chunks = cells // CHUNK
    fr = 4 * nf
    hr = 2 * nf

    f_copies = halo(0, fields.at[0, :, 0], fields.at[0, :, 1], f_land)

    win_t[...] = jnp.zeros_like(win_t)
    for k in range(27):
        win_t[k * nf : (k + 1) * nf, 0:c1] = w_in[k].astype(F32)
    flat = win_t[...].T[0:c1, :].astype(BF)
    spread_w = dot(flat, fold[...]).astype(BF)
    for m in range(8):
        win[m * c1 : (m + 1) * c1, :] = spread_w[:, m * 64 * nf : (m + 1) * 64 * nf]
        wdt[m * c1 : (m + 1) * c1, :] = w_dn[part_of(m)]
        wu[m * c1 : (m + 1) * c1, :] = w_up[part_of(m)]
    wd[...] = wdt[...].astype(F32).T.astype(BF)
    wut[...] = wu[...].astype(F32).T.astype(BF)
    bd[...] = jnp.zeros_like(bd)
    for m in range(8):
        bd[m * nf : (m + 1) * nf, m * c1 : (m + 1) * c1] = w_out[...].astype(F32)
    bdt[...] = bd[...].T.astype(BF)
    bd_b = bd[...].astype(BF)
    for q in range(3):
        for a in range(3):
            wf[q, :, a * c2 : (a + 1) * c2] = jnp.concatenate(
                [w_co[9 * a + 3 * q + b] for b in range(3)], axis=0
            ).astype(F32)
            for b in range(3):
                wa[q, a * c2 : (a + 1) * c2, b * c2 : (b + 1) * c2] = w_co[
                    9 * (2 - a) + 3 * (2 - q) + b
                ].astype(F32)
        wb[q] = wa[q].T.astype(BF)

    cot_rows = cot[0].astype(F32).reshape(2 * nf * ny, nz).astype(BF)
    cot_t[...] = dot(dot(perm2[...], cot_rows).astype(BF), split[:, LANES : 3 * LANES]).astype(BF)
    for y in range(yc):
        for m in range(2):
            cots[m * 2 * hr : (m + 1) * 2 * hr, y * LANES : (y + 1) * LANES] = cot_t[
                y * 2 * hr : (y + 1) * 2 * hr, m * LANES : (m + 1) * LANES
            ]
    for n in range(chunks):
        at = slice(n * CHUNK, (n + 1) * CHUNK)
        back = dot(bdt[...], cots[:, at]).astype(BF)
        bm[:, at] = back
        term[:, at] = dot(wut[...], back)

    rows = nf * ny
    ff[0 : 2 * rows, :] = fields[0].astype(F32).reshape(2 * rows, nz).astype(BF)
    finish(f_copies)
    ff[2 * rows : 3 * rows, :] = (f_land[0].astype(F32).reshape(rows, nz) * has_left).astype(BF)
    ff[3 * rows : 4 * rows, :] = (f_land[1].astype(F32).reshape(rows, nz) * has_right).astype(BF)
    tt[...] = dot(dot(perm[...], ff[...]).astype(BF), split[...]).astype(BF)
    for y in range(yc):
        for dy in range(4):
            for dz in range(4):
                patches[(dy * 4 + dz) * fr : (dy * 4 + dz + 1) * fr, y * LANES : (y + 1) * LANES] = tt[
                    (2 * y + dy) * fr : (2 * y + dy + 1) * fr, dz * LANES : (dz + 1) * LANES
                ]
    for n in range(chunks):
        at = slice(n * CHUNK, (n + 1) * CHUNK)
        pre = dot(win[...], patches[:, at])
        sigma = jax.nn.sigmoid(pre)
        fine = (pre * sigma).astype(BF)
        slope[:, at] = sigma * (1.0 + pre * (1.0 - sigma))
        act[:, at] = fine
        red_out[:, at] = dot(wd[...], fine).astype(BF)
    r_copies = halo(1, red_out, red_out, r_land)
    edge = jnp.zeros((3 * c2, LANES), BF)
    for planes in (red, bc):
        planes[:, 0:LANES] = edge
        planes[:, LANES + cells : 2 * LANES + cells] = edge
    inner = slice(LANES, LANES + cells)
    red[c2 : 2 * c2, inner] = red_out[...]
    finish(r_copies)
    red[0:c2, inner] = (r_land[0].astype(F32) * has_left).astype(BF)
    red[2 * c2 : 3 * c2, inner] = (r_land[1].astype(F32) * has_right).astype(BF)

    lane = lax.rem(lax.broadcasted_iota(jnp.int32, (c2, CHUNK), 1), LANES)
    not_first, not_last = lane > 0, lane < LANES - 1

    def later(v):
        return jnp.where(not_first, pltpu.roll(v, 1, 1), 0.0)

    def sooner(v):
        return jnp.where(not_last, pltpu.roll(v, CHUNK - 1, 1), 0.0)

    wf_b = [wf[q].astype(BF) for q in range(3)]

    for n in range(chunks):
        at = slice(n * CHUNK, (n + 1) * CHUNK)
        out = sum(
            dot(wf_b[q], red[:, n * CHUNK + q * LANES : (n + 1) * CHUNK + q * LANES])
            for q in range(3)
        )
        pre = out[c2 : 2 * c2] + later(out[0:c2]) + sooner(out[2 * c2 : 3 * c2])
        sigma = jax.nn.sigmoid(pre)
        act_c[:, at] = (pre * sigma).astype(BF)
        back = (term[:, at] * (sigma * (1.0 + pre * (1.0 - sigma)))).astype(BF)
        bc_out[:, at] = back
        wide = back.astype(F32)
        rolled[0:c2, at] = sooner(wide).astype(BF)
        rolled[c2 : 2 * c2, at] = back
        rolled[2 * c2 : 3 * c2, at] = later(wide).astype(BF)
    b_copies = halo(2, bc_out, bc_out, b_land)
    bc[c2 : 2 * c2, inner] = bc_out[...]

    for q in range(3):
        gc[q * 3 * c2 : (q + 1) * 3 * c2, :] = dot_nt(
            rolled[...], red[:, q * LANES : q * LANES + cells]
        )
    g_out_wide = jnp.zeros((8 * nf, 8 * c1), F32)
    for n in range(chunks):
        at = slice(n * CHUNK, (n + 1) * CHUNK)
        merged = (act[:, at].astype(F32) + dot(wu[...], act_c[:, at])).astype(BF)
        out = dot(bd_b, merged).astype(BF)
        g_out_wide = g_out_wide + dot_nt(cots[:, at], merged)
        for y in range(CHUNK // LANES):
            for m in range(2):
                pred_t[
                    (n * (CHUNK // LANES) + y) * 2 * hr : (n * (CHUNK // LANES) + y + 1) * 2 * hr,
                    m * LANES : (m + 1) * LANES,
                ] = out[m * 2 * hr : (m + 1) * 2 * hr, y * LANES : (y + 1) * LANES]
    gu = dot_nt(bm[...], act_c[...])
    mine = (
        lax.broadcasted_iota(jnp.int32, (8 * nf, 8 * c1), 0) // nf
        == lax.broadcasted_iota(jnp.int32, (8 * nf, 8 * c1), 1) // c1
    )
    g_out_wide = jnp.where(mine, g_out_wide, 0.0)
    g_out_half = g_out_wide[:, 0:LANES] + g_out_wide[:, LANES : 2 * LANES]
    g_out_half = g_out_half + pltpu.roll(g_out_half, 64, 1)
    g_out_half = g_out_half + pltpu.roll(g_out_half, 32, 1)
    g_out_half = g_out_half[0:8] + g_out_half[8:16] + g_out_half[16:24] + g_out_half[24:32]
    g_out_half = g_out_half + pltpu.roll(g_out_half, 4, 0)

    e_rows = e_send.shape[1]
    full[0 : 9 * c2, :] = gc[:, 0:LANES]
    half = 9 * c2 // 2
    full[9 * c2 : 9 * c2 + half, 0:c2] = gc[0:half, LANES : LANES + c2]
    full[9 * c2 : 9 * c2 + half, c2 : 2 * c2] = gc[half : 2 * half, LANES : LANES + c2]
    up_at = 9 * c2 + half
    full[up_at : up_at + LANES, 0:c2] = gu[0:LANES]
    full[up_at : up_at + LANES, c2 : 2 * c2] = gu[LANES : 2 * LANES]
    out_at = up_at + LANES
    full[out_at : out_at + 8, :] = g_out_half
    full[out_at + 8 : out_at + 32, :] = jnp.zeros((24, LANES), F32)
    e_send[...] = full[...].reshape(nxy, e_rows, LANES).astype(BF)

    def plane_copy(i, src, dst, send_sem, recv_sem):
        return pltpu.make_async_remote_copy(
            src_ref=src, dst_ref=dst, send_sem=send_sem, recv_sem=recv_sem,
            device_id=plane_peer(i)[1], device_id_type=MESH,
        )

    def send_early(i, carry):
        plane_copy(i, e_send.at[plane_peer(i)[0]], e_recv.at[i], e_ss, e_rs).start()
        return carry

    lax.fori_loop(1, nxy, send_early, 0)
    e_recv[0] = e_send[me]

    finish(b_copies)
    bc[0:c2, inner] = (b_land[0].astype(F32) * has_left).astype(BF)
    bc[2 * c2 : 3 * c2, inner] = (b_land[1].astype(F32) * has_right).astype(BF)
    for n in range(chunks):
        at = slice(n * CHUNK, (n + 1) * CHUNK)
        out = sum(
            dot(wb[q], bc[:, n * CHUNK + q * LANES : (n + 1) * CHUNK + q * LANES])
            for q in range(3)
        )
        back = out[c2 : 2 * c2] + sooner(out[0:c2]) + later(out[2 * c2 : 3 * c2])
        back = back.astype(BF)
        bc_out_at = rolled
        bc_out_at[0:c2, at] = back
        bf[:, at] = ((bm[:, at].astype(F32) + dot(wdt[...], back)) * slope[:, at]).astype(BF)
    gd = dot_nt(act[...], rolled[0:c2, :])
    late[0:LANES, 0:c2] = gd[0:LANES]
    late[0:LANES, c2 : 2 * c2] = gd[LANES : 2 * LANES]
    gi = dot_nt(bf[...], patches[...]).astype(BF)
    for m in range(8):
        gi_wide[:, m * 64 * nf : (m + 1) * 64 * nf] = gi[m * c1 : (m + 1) * c1, :]
    late[LANES : LANES + c1, :] = dot_nt(gi_wide[...], fold[...])
    l_rows = (LANES + c1) // nxy
    for p in range(nxy):
        l_send[p, 0:l_rows, :] = late[p * l_rows : (p + 1) * l_rows, :]

    def send_late(i, carry):
        plane_copy(i, l_send.at[plane_peer(i)[0]], l_recv.at[i], l_ss, l_rs).start()
        return carry

    lax.fori_loop(1, nxy, send_late, 0)
    l_recv[0] = l_send[me]

    out = dot(dot(perm2t[...], pred_t[...]).astype(BF), join[...])
    pred[0] = out.reshape(nf, 2, ny, nz).astype(BF)

    def all_of(ref, sem, count):
        block = ref.at[pl.ds(0, count)]
        pltpu.make_async_copy(block, block, sem).wait()

    all_of(e_recv, e_rs, nxy - 1)
    early_sum = jnp.sum(e_recv[...].astype(F32), axis=0)
    all_of(l_recv, l_rs, nxy - 1)
    late_sum = jnp.sum(l_recv[...], axis=0)

    z_rows = -(-(e_rows + l_rows) // nzg)
    full[0:e_rows, :] = early_sum
    full[e_rows : e_rows + l_rows, :] = late_sum[0:l_rows]
    for j in range(nzg):
        z_send[j, 0:z_rows, :] = full[j * z_rows : (j + 1) * z_rows, :]

    def send_z(i, carry):
        peer, device = z_peer(i)
        pltpu.make_async_remote_copy(
            src_ref=z_send.at[peer], dst_ref=z_recv.at[i], send_sem=z_ss, recv_sem=z_rs,
            device_id=device, device_id_type=MESH,
        ).start()
        return carry

    lax.fori_loop(1, nzg, send_z, 0)
    z_recv[0] = z_send[zi]
    all_of(z_recv, z_rs, nzg - 1)
    total = jnp.sum(z_recv[...], axis=0)
    z_out[...] = total
    z_all[zi] = total

    def spread_z(i, carry):
        pltpu.make_async_remote_copy(
            src_ref=z_out, dst_ref=z_all.at[zi], send_sem=y_ss, recv_sem=y_rs,
            device_id=z_peer(i)[1], device_id_type=MESH,
        ).start()
        return carry

    lax.fori_loop(1, nzg, spread_z, 0)
    all_of(z_all, y_rs, nzg - 1)
    for j in range(nzg):
        full[j * z_rows : (j + 1) * z_rows, :] = z_all[j, 0:z_rows, :]
    e_out[...] = full[0:e_rows, :].astype(BF)
    l_out[0:l_rows, :] = full[e_rows : e_rows + l_rows, :]
    e_all[me] = e_out[...]
    l_all[me] = l_out[...]

    def spread_plane(i, carry):
        plane_copy(i, e_out, e_all.at[me], a_ss, a_rs).start()
        plane_copy(i, l_out, l_all.at[me], b_ss, b_rs).start()
        return carry

    lax.fori_loop(1, nxy, spread_plane, 0)

    all_of(e_send, e_ss, nxy - 1)
    all_of(l_send, l_ss, nxy - 1)
    all_of(z_send, z_ss, nzg - 1)
    all_of(z_all, y_ss, nzg - 1)
    all_of(e_all, a_rs, nxy - 1)
    all_of(l_all, b_rs, nxy - 1)
    all_of(e_all, a_ss, nxy - 1)
    all_of(l_all, b_ss, nxy - 1)

    full[...] = e_all[...].astype(F32).reshape(nxy * e_rows, LANES)
    for q in range(3):
        for b in range(3):
            row = (q * 3 + b) * c2
            block = full[row : row + c2, :]
            g_co[3 * q + b] = block[:, 0:c2]
            g_co[9 + 3 * q + b] = pltpu.roll(block, c2, 1)[:, 0:c2]
    for n in range(9):
        row = 9 * c2 + (n * c2) % half
        lo = min(c2, half - (n * c2) % half)
        first, side = n * c2 // half, None
        block = full[row : row + lo, :]
        if first == 1:
            block = pltpu.roll(block, c2, 1)
        g_co[18 + n, 0:lo, :] = block[:, 0:c2]
        if lo < c2:
            rest = pltpu.roll(full[9 * c2 : 9 * c2 + c2 - lo, :], c2, 1)
            g_co[18 + n, lo:c2, :] = rest[:, 0:c2]
    for m in range(4):
        block = full[up_at + m * c1 : up_at + (m + 1) * c1, :]
        g_up[part_of(m)] = block[:, 0:c2]
        g_up[part_of(m + 4)] = pltpu.roll(block, c2, 1)[:, 0:c2]
    g_out[...] = full[out_at : out_at + nf, 0:c1]
    for p in range(nxy):
        late[p * l_rows : (p + 1) * l_rows, :] = l_all[p, 0:l_rows, :]
    for m in range(4):
        block = late[m * c1 : (m + 1) * c1, :]
        g_dn[part_of(m)] = block[:, 0:c2]
        g_dn[part_of(m + 4)] = pltpu.roll(block, c2, 1)[:, 0:c2]
    win_t[0:c1, :] = late[LANES : LANES + c1, :]
    flipped = win_t[...].T
    for k in range(27):
        g_in[k] = flipped[k * nf : (k + 1) * nf, 0:c1]


def shards(fields, cotangent, w_in, w_down, w_coarse, w_up, w_out):
    ns, nspace = lax.axis_size("sample"), lax.axis_size("space")
    nf, ny, nz = fields.shape[1], fields.shape[3], fields.shape[4]
    c1, c2 = w_up.shape[1], w_up.shape[2]
    cells = (ny // 2) * (nz // 2)
    nxy, nzg = ns * HIGH, nspace // HIGH
    e_rows = (9 * c2 * 3 // 2 + LANES + 32) // nxy
    l_rows = (LANES + c1) // nxy
    z_rows = -(-(e_rows + l_rows) // nzg)
    zr = -(-z_rows // 4) * 4 if z_rows > 4 else 4
    if zr > 4:
        zr = -(-zr // 8) * 8
    lr = -(-l_rows // 8) * 8
    wide = 64 * nf
    consts = one_hots(ny, nz, nf)
    vm = pltpu.VMEM
    dma = pltpu.SemaphoreType.DMA
    scratch = [
        vm((2, nf, ny, nz), BF),
        vm((4 * nf * ny, nz), BF),
        vm(((ny + 2) * 4 * nf, 4 * LANES), BF),
        vm((wide, cells), BF),
        vm((8 * c1, wide), BF),
        vm((128, 128), F32),
        vm((8 * c1, c2), BF),
        vm((c2, 8 * c1), BF),
        vm((8 * c1, c2), BF),
        vm((c2, 8 * c1), BF),
        vm((8 * nf, 8 * c1), F32),
        vm((8 * c1, 8 * nf), BF),
        vm((3, 3 * c2, 3 * c2), F32),
        vm((3, 3 * c2, 3 * c2), BF),
        vm((3, 3 * c2, 3 * c2), F32),
        vm((8 * c1, cells), BF),
        vm((8 * c1, cells), F32),
        vm((8 * nf, cells), BF),
        vm((2 * nf * ny, 2 * LANES), BF),
        vm((8 * c1, cells), BF),
        vm((c2, cells), F32),
        vm((3 * c2, cells + 2 * LANES), BF),
        vm((2, c2, cells), BF),
        vm((3 * c2, cells + 2 * LANES), BF),
        vm((2, c2, cells), BF),
        vm((3 * c2, cells), BF),
        vm((c2, cells), BF),
        vm((2 * nf * ny, 2 * LANES), BF),
        vm((8 * c1, cells), BF),
        vm((c2, cells), BF),
        vm((c2, cells), BF),
        vm((c1, 8 * wide), BF),
        vm((9 * c2, 3 * c2), F32),
        vm((nxy, e_rows, LANES), BF),
        vm((nxy, e_rows, LANES), BF),
        vm((nxy, lr, LANES), F32),
        vm((nxy, lr, LANES), F32),
        vm((LANES + c1, LANES), F32),
        vm((nzg, zr, LANES), F32),
        vm((nzg, zr, LANES), F32),
        vm((zr, LANES), F32),
        vm((nzg, zr, LANES), F32),
        vm((e_rows, LANES), BF),
        vm((nxy, e_rows, LANES), BF),
        vm((lr, LANES), F32),
        vm((nxy, lr, LANES), F32),
        vm((nxy * e_rows, LANES), F32),
        dma((6,)), dma((6,)),
    ] + [dma] * 12
    shape = jax.ShapeDtypeStruct
    whole = pl.BlockSpec(memory_space=pltpu.VMEM)
    outs = pl.pallas_call(
        functools.partial(body, ns, nspace),
        out_shape=(
            shape(fields.shape, BF),
            shape((27, nf, c1), F32),
            shape((8, c1, c2), F32),
            shape((27, c2, c2), F32),
            shape((8, c1, c2), F32),
            shape((nf, c1), F32),
        ),
        in_specs=[whole] * 13,
        out_specs=[whole] * 6,
        scratch_shapes=scratch,
        compiler_params=pltpu.CompilerParams(
            collective_id=0, has_side_effects=True, vmem_limit_bytes=48 * 2**20
        ),
        name="unet_block",
    )(
        fields, cotangent, w_in.transpose(0, 2, 1), w_down.transpose(0, 2, 1), w_coarse, w_up,
        w_out, *consts,
    )
    prediction, g_in, g_dn, g_co, g_up, g_out = outs
    return (prediction, g_in.transpose(0, 2, 1), g_dn.transpose(0, 2, 1), g_co, g_up, g_out)


def solution(mesh):
    split = P("sample", None, "space", None, None)
    return jax.shard_map(
        shards,
        mesh=mesh,
        in_specs=(split, split, P(), P(), P(), P(), P()),
        out_specs=(split, P(), P(), P(), P(), P()),
        check_vma=False,
    )
```

time: 616 us -> 86 us (0.14)
  waiting for transfers between devices: 360 us -> 0 us
  blocking collectives: 119 us -> 0 us
  Pallas kernels: 0 us -> 69.1 us
  local copies, waits for them, and re-layouts: 69.6 us -> 15.6 us
  matrix products: 29.4 us -> 0 us
  starting transfers between devices: 18.4 us -> 0 us
  between operations: 14.6 us -> 0.67 us
    psum x1 -> x0, waiting for transfers between devices: 358 us -> none  [reduce_term(): return lax.psum(term, ('sample', 'space'))]
    psum x1 -> x0, blocking collectives: 119 us -> none  [reduce_term(): return lax.psum(term, ('sample', 'space'))]
    pallas_call x0 -> x1, Pallas kernels: none -> 69.1 us  [shards(): pl.pallas_call(functools.partial(body, ns, nspace), out_shape=(shape(fiel...]
    another operation x33 -> x0, local copies, waits for them, and re-layouts: 31.4 us -> none  [the longest x29 28.8 us: all_taps(): return jnp.stack(windows)]
    dot_general x38 -> x0, matrix products: 29.4 us -> none  [the longest x9 8.53 us: weight_grad_rows(): jnp.einsum('oxyz,tcxyz->toc', gradient, window, preferred_element_type=jn...]
    ppermute x6 -> x0, starting transfers between devices: 18.3 us -> none  [the longest x3 14.3 us: with_halo(): lax.ppermute(tail, axis, [(i, (i + 1) % count) for i in range(ends)])]
    transpose x2 -> x0, local copies, waits for them, and re-layouts: 12.8 us -> none  [the longest x1 6.41 us: shards(): jnp.einsum('ijkoc,oxyz->cxiyjzk', down_five, back_reduced, preferred_elem...]
    reshape x2 -> x0, local copies, waits for them, and re-layouts: 10.1 us -> none  [the longest x1 5.71 us: shards(): spread = jnp.einsum('ijkoc,oxyz->cxiyjzk', down_five, back_reduced, prefe...]
  transfers between devices with their start and end apart: 7 -> 0, of which waited for: 2 -> 0; matrix products, arithmetic and copies ran while one was open for 5% -> 0% of each run, Pallas kernels for 0% -> 0%
where the time goes in v1:
time: 86 us; the launch traced here: 85.4 us
  Pallas kernels  69.1 us (80%)
  local copies, waits for them, and re-layouts  15.6 us (18%)
    pallas_call x1, Pallas kernels, shards(): pl.pallas_call(functools.partial(body, ns, nspace), out_shape=(shape(fiel...  69.1 us
    unnamed x32, local copies, waits for them, and re-layouts  15.6 us

profile of v1, /device:TPU:1, one launch (start us, length us, event | category | flops | bytes accessed | tf_op | source)
XLA Modules:
  0.0 85.4 jit_solution(10517697989957840791)
XLA Ops:
  0.6 0.0 copy-start.12
  0.6 0.7 copy-done.12
  1.3 0.0 copy-start
  1.3 1.0 %copy-done = bf16[128,2048]{1,0:T(8,128)(2,1)S(1)} copy-done((bf16[128,2048]{1,0:T(8,128)(2,1)S(1)}, bf16[128,2048]{1,0:T(8,128)(2,1)}, u32[]{:S(2)}) %copy-start) | copy-done | bytes 524312
  2.4 0.0 copy-start.1
  2.4 1.0 %copy-done.1 = bf16[27,64,64]{2,1,0:T(8,128)(2,1)S(1)} copy-done((bf16[27,64,64]{2,1,0:T(8,128)(2,1)S(1)}, bf16[27,64,64]{2,1,0:T(8,128)(2,1)}, u32[]{:S(2)}) %copy-start.1) | copy-done | bytes 221208
  3.4 0.0 copy-start.2
  3.4 1.0 %copy-done.2 = bf16[416,384]{1,0:T(8,128)(2,1)S(1)} copy-done((bf16[416,384]{1,0:T(8,128)(2,1)S(1)}, bf16[416,384]{1,0:T(8,128)(2,1)}, u32[]{:S(2)}) %copy-start.2) | copy-done | bytes 319512
  4.3 0.9 %copy-done.3 = bf16[256,512]{1,0:T(8,128)(2,1)S(1)} copy-done((bf16[256,512]{1,0:T(8,128)(2,1)S(1)}, bf16[256,512]{1,0:T(8,128)(2,1)}, u32[]{:S(2)}) %copy-start.3) | copy-done | bytes 262168
  5.3 0.9 %copy-done.4 = bf16[256,256]{1,0:T(8,128)(2,1)S(1)} copy-done((bf16[256,256]{1,0:T(8,128)(2,1)S(1)}, bf16[256,256]{1,0:T(8,128)(2,1)}, u32[]{:S(2)}) %copy-start.4) | copy-done | bytes 131096
  6.2 0.9 %copy-done.5 = bf16[1,4,2,24,256]{4,3,2,1,0:T(8,128)(2,1)S(1)} copy-done((bf16[1,4,2,24,256]{4,3,2,1,0:T(8,128)(2,1)S(1)}, bf16[1,4,2,24,256]{4,3,2,1,0:T(8,128)(2,1)}, u32[]{:S(2)}) %copy-start.5) | copy-done | bytes 98328
  7.1 0.9 %copy-done.6 = bf16[1,4,2,24,256]{4,3,2,1,0:T(8,128)(2,1)S(1)} copy-done((bf16[1,4,2,24,256]{4,3,2,1,0:T(8,128)(2,1)S(1)}, bf16[1,4,2,24,256]{4,3,2,1,0:T(8,128)(2,1)}, u32[]{:S(2)}) %copy-start.6) | copy-done | bytes 98328
  8.0 0.9 %copy-done.7 = bf16[192,192]{1,0:T(8,128)(2,1)S(1)} copy-done((bf16[192,192]{1,0:T(8,128)(2,1)S(1)}, bf16[192,192]{1,0:T(8,128)(2,1)}, u32[]{:S(2)}) %copy-start.7) | copy-done | bytes 73752
  8.9 0.9 %copy-done.8 = bf16[192,192]{1,0:T(8,128)(2,1)S(1)} copy-done((bf16[192,192]{1,0:T(8,128)(2,1)S(1)}, bf16[192,192]{1,0:T(8,128)(2,1)}, u32[]{:S(2)}) %copy-start.8) | copy-done | bytes 73752
  9.8 0.8 copy-done.9
  10.6 0.8 copy-done.10
  11.5 0.7 copy-done.11
  12.2 69.1 %unet_block.1 = (bf16[1,4,2,24,256]{4,3,2,1,0:T(8,128)(2,1)S(1)}, f32[27,4,32]{2,1,0:T(4,128)S(1)}, f32[8,32,64]{2,1,0:T(8,128)S(1)}, f32[27,64,64]{2,1,0:T(8,12...) custom-call(bf16[1,4,2,24,256]{4,3,2,1,0:T(8,128)(2,1)S(1)} %copy-done.5, ...), custom_call_target="tpu_custom_call" | custom-call | tf_op jit(solution)/shard_map/unet_block/pallas_call | solution.py:501
  81.3 0.6 copy.25
  82.0 0.6 copy.26
  82.6 0.7 copy.27
  83.3 0.9 %copy.28 = f32[27,64,64]{2,1,0:T(8,128)} copy(f32[27,64,64]{2,1,0:T(8,128)S(1)} %get-tuple-element.27) | data formatting | bytes 884736
  84.2 0.7 copy.29
  84.8 0.6 copy.30
  (9 shorter events, 0.0 us)
Async XLA Ops:
  0.6 0.7 copy-start.12
  1.3 1.0 %copy-start = (bf16[128,2048]{1,0:T(8,128)(2,1)S(1)}, bf16[128,2048]{1,0:T(8,128)(2,1)}, u32[]{:S(2)}) copy-start(bf16[128,2048]{1,0:T(8,128)(2,1)} %constant.17.clone.fold) | copy-start | bytes 1572868
  2.4 1.0 %copy-start.1 = (bf16[27,64,64]{2,1,0:T(8,128)(2,1)S(1)}, bf16[27,64,64]{2,1,0:T(8,128)(2,1)}, u32[]{:S(2)}) copy-start(bf16[27,64,64]{2,1,0:T(8,128)(2,1)} %w_co.1) | copy-start | bytes 663556
  3.4 1.0 %copy-start.2 = (bf16[416,384]{1,0:T(8,128)(2,1)S(1)}, bf16[416,384]{1,0:T(8,128)(2,1)}, u32[]{:S(2)}) copy-start(bf16[416,384]{1,0:T(8,128)(2,1)} %constant.12.clone.perm) | copy-start | bytes 958468
  4.3 0.9 %copy-start.3 = (bf16[256,512]{1,0:T(8,128)(2,1)S(1)}, bf16[256,512]{1,0:T(8,128)(2,1)}, u32[]{:S(2)}) copy-start(bf16[256,512]{1,0:T(8,128)(2,1)} %constant.15.clone.split) | copy-start | bytes 786436
  5.3 0.9 %copy-start.4 = (bf16[256,256]{1,0:T(8,128)(2,1)S(1)}, bf16[256,256]{1,0:T(8,128)(2,1)}, u32[]{:S(2)}) copy-start(bf16[256,256]{1,0:T(8,128)(2,1)} %constant.16.clone.join) | copy-start | bytes 393220
  6.2 0.9 %copy-start.5 = (bf16[1,4,2,24,256]{4,3,2,1,0:T(8,128)(2,1)S(1)}, bf16[1,4,2,24,256]{4,3,2,1,0:T(8,128)(2,1)}, u32[]{:S(2)}) copy-start(bf16[1,4,2,24,256]{4,3,2,1,0:T(8,128)(2,1)} %fields.1) | copy-start | bytes 294916
  7.1 0.9 %copy-start.6 = (bf16[1,4,2,24,256]{4,3,2,1,0:T(8,128)(2,1)S(1)}, bf16[1,4,2,24,256]{4,3,2,1,0:T(8,128)(2,1)}, u32[]{:S(2)}) copy-start(bf16[1,4,2,24,256]{4,3,2,1,0:T(8,128)(2,1)} %cot.1) | copy-start | bytes 294916
  8.0 0.9 %copy-start.7 = (bf16[192,192]{1,0:T(8,128)(2,1)S(1)}, bf16[192,192]{1,0:T(8,128)(2,1)}, u32[]{:S(2)}) copy-start(bf16[192,192]{1,0:T(8,128)(2,1)} %constant.14.clone.perm2t) | copy-start | bytes 221188
  8.9 0.9 %copy-start.8 = (bf16[192,192]{1,0:T(8,128)(2,1)S(1)}, bf16[192,192]{1,0:T(8,128)(2,1)}, u32[]{:S(2)}) copy-start(bf16[192,192]{1,0:T(8,128)(2,1)} %constant.13.clone.perm2) | copy-start | bytes 221188
  9.8 0.8 copy-start.9
  10.6 0.8 copy-start.10
  11.4 0.7 copy-start.11

commit v2 on v1

--- a/solution.py
+++ b/solution.py
@@ -13,6 +13,7 @@
 F32 = jnp.float32
 LANES = 128
 CHUNK = 256
+VMEM = 63 * 2**20
 HIGH = 2
 
 
@@ -66,15 +67,24 @@
 
 def body(
     ns, nspace,
-    fields, cot, w_in, w_dn, w_co, w_up, w_out, perm, perm2, perm2t, split, join, fold,
-    pred, g_in, g_dn, g_co, g_up, g_out,
+    *refs,
+):
+    given, results, inputs, rest = refs[:13], refs[13:19], refs[19:32], refs[32:]
+    work(ns, nspace, given, results, inputs, *rest)
+
+
+def work(
+    ns, nspace, given, results, inputs,
     f_land, ff, tt, patches, win, win_t, wdt, wd, wu, wut, bd, bdt, wf, wb, wa,
     act, slope, cots, cot_t, bm, term, red, r_land, bc, b_land, rolled, act_c, pred_t, bf,
     red_out, bc_out,
-    gi_wide, gc, e_send, e_recv, l_send, l_recv, late, z_send, z_recv, z_out, z_all,
+    gi_wide, gc, e_rest, e_send, e_recv, l_send, l_recv, late, ez_out, ez_all, lz_out, lz_all,
     e_out, e_all, l_out, l_all, full,
-    halo_ss, halo_rs, e_ss, e_rs, l_ss, l_rs, z_ss, z_rs, y_ss, y_rs, a_ss, a_rs, b_ss, b_rs,
+    in_s, halo_ss, halo_rs,
+    e_ss, e_rs, l_ss, l_rs, z_ss, z_rs, y_ss, y_rs, a_ss, a_rs, b_ss, b_rs,
 ):
+    fields, cot, w_in, w_dn, w_co, w_up, w_out, perm, perm2, perm2t, split, join, fold = inputs
+    pred, g_in, g_dn, g_co, g_up, g_out = results
     nzg = nspace // HIGH
     nxy = ns * HIGH
     s = lax.axis_index("sample")
@@ -99,29 +109,37 @@
     def greet(device):
         pl.semaphore_signal(barrier, inc=1, device_id=device, device_id_type=MESH)
 
-    greet((s, left))
-    greet((s, right))
-
     def greet_plane(i, carry):
         greet(plane_peer(i)[1])
         return carry
 
-    def greet_z(i, carry):
-        greet(z_peer(i)[1])
+    def greet_far(i, carry):
+        greet(z_peer(nzg // 2 + i)[1])
+        greet(z_peer(nzg // 2 - i)[1])
         return carry
 
+    greet(z_peer(nzg // 2)[1])
+    lax.fori_loop(1, nzg // 2, greet_far, 0)
     lax.fori_loop(1, nxy, greet_plane, 0)
-    lax.fori_loop(1, nzg, greet_z, 0)
+    greet((s, left))
+    greet((s, right))
+    loads = [
+        pltpu.make_async_copy(src, dst, in_s.at[i])
+        for i, (src, dst) in enumerate(zip(given, inputs))
+    ]
+    for i in (0, 2, 12, 3, 5, 6, 4, 1, 8, 10, 7, 9, 11):
+        loads[i].start()
+    loads[0].wait()
     pl.semaphore_wait(barrier, 2 + nxy - 1 + nzg - 1)
 
-    def halo(step, to_left, to_right, land):
+    def halo(step, to_left, to_right, from_left, from_right):
         copies = [
             pltpu.make_async_remote_copy(
-                src_ref=to_right, dst_ref=land.at[0], send_sem=halo_ss.at[2 * step],
+                src_ref=to_right, dst_ref=from_left, send_sem=halo_ss.at[2 * step],
                 recv_sem=halo_rs.at[2 * step], device_id=(s, right), device_id_type=MESH,
             ),
             pltpu.make_async_remote_copy(
-                src_ref=to_left, dst_ref=land.at[1], send_sem=halo_ss.at[2 * step + 1],
+                src_ref=to_left, dst_ref=from_right, send_sem=halo_ss.at[2 * step + 1],
                 recv_sem=halo_rs.at[2 * step + 1], device_id=(s, left), device_id_type=MESH,
             ),
         ]
@@ -141,7 +159,15 @@
     fr = 4 * nf
     hr = 2 * nf
 
-    f_copies = halo(0, fields.at[0, :, 0], fields.at[0, :, 1], f_land)
+    def halo_chunk(step, n, src, land):
+        at = pl.ds(n * CHUNK, CHUNK)
+        return halo(
+            step * chunks + n + 1, src.at[:, at], src.at[:, at], land.at[0, :, at], land.at[1, :, at]
+        )
+
+    f_copies = halo(0, fields.at[0, :, 0], fields.at[0, :, 1], f_land.at[0], f_land.at[1])
+    for i in (2, 12, 3, 5, 6, 4):
+        loads[i].wait()
 
     win_t[...] = jnp.zeros_like(win_t)
     for k in range(27):
@@ -170,6 +196,8 @@
                 ].astype(F32)
         wb[q] = wa[q].T.astype(BF)
 
+    for i in (1, 8, 10, 7, 9, 11):
+        loads[i].wait()
     cot_rows = cot[0].astype(F32).reshape(2 * nf * ny, nz).astype(BF)
     cot_t[...] = dot(dot(perm2[...], cot_rows).astype(BF), split[:, LANES : 3 * LANES]).astype(BF)
     for y in range(yc):
@@ -195,6 +223,7 @@
                 patches[(dy * 4 + dz) * fr : (dy * 4 + dz + 1) * fr, y * LANES : (y + 1) * LANES] = tt[
                     (2 * y + dy) * fr : (2 * y + dy + 1) * fr, dz * LANES : (dz + 1) * LANES
                 ]
+    r_copies = []
     for n in range(chunks):
         at = slice(n * CHUNK, (n + 1) * CHUNK)
         pre = dot(win[...], patches[:, at])
@@ -203,16 +232,21 @@
         slope[:, at] = sigma * (1.0 + pre * (1.0 - sigma))
         act[:, at] = fine
         red_out[:, at] = dot(wd[...], fine).astype(BF)
-    r_copies = halo(1, red_out, red_out, r_land)
+        r_copies.append(halo_chunk(0, n, red_out, r_land))
     edge = jnp.zeros((3 * c2, LANES), BF)
     for planes in (red, bc):
         planes[:, 0:LANES] = edge
         planes[:, LANES + cells : 2 * LANES + cells] = edge
     inner = slice(LANES, LANES + cells)
     red[c2 : 2 * c2, inner] = red_out[...]
-    finish(r_copies)
-    red[0:c2, inner] = (r_land[0].astype(F32) * has_left).astype(BF)
-    red[2 * c2 : 3 * c2, inner] = (r_land[1].astype(F32) * has_right).astype(BF)
+
+    def arrive(n, copies, land, planes):
+        finish(copies[n])
+        at = slice(n * CHUNK, (n + 1) * CHUNK)
+        there = slice(LANES + n * CHUNK, LANES + (n + 1) * CHUNK)
+        planes[0:c2, there] = (land[0, :, at].astype(F32) * has_left).astype(BF)
+        planes[2 * c2 : 3 * c2, there] = (land[1, :, at].astype(F32) * has_right).astype(BF)
+
 
     lane = lax.rem(lax.broadcasted_iota(jnp.int32, (c2, CHUNK), 1), LANES)
     not_first, not_last = lane > 0, lane < LANES - 1
@@ -225,7 +259,11 @@
 
     wf_b = [wf[q].astype(BF) for q in range(3)]
 
+    b_copies = []
+    arrive(0, r_copies, r_land, red)
     for n in range(chunks):
+        if n + 1 < chunks:
+            arrive(n + 1, r_copies, r_land, red)
         at = slice(n * CHUNK, (n + 1) * CHUNK)
         out = sum(
             dot(wf_b[q], red[:, n * CHUNK + q * LANES : (n + 1) * CHUNK + q * LANES])
@@ -236,17 +274,38 @@
         act_c[:, at] = (pre * sigma).astype(BF)
         back = (term[:, at] * (sigma * (1.0 + pre * (1.0 - sigma)))).astype(BF)
         bc_out[:, at] = back
+        b_copies.append(halo_chunk(1, n, bc_out, b_land))
         wide = back.astype(F32)
         rolled[0:c2, at] = sooner(wide).astype(BF)
         rolled[c2 : 2 * c2, at] = back
         rolled[2 * c2 : 3 * c2, at] = later(wide).astype(BF)
-    b_copies = halo(2, bc_out, bc_out, b_land)
     bc[c2 : 2 * c2, inner] = bc_out[...]
 
     for q in range(3):
         gc[q * 3 * c2 : (q + 1) * 3 * c2, :] = dot_nt(
             rolled[...], red[:, q * LANES : q * LANES + cells]
         )
+    def plane_copy(i, src, dst, send_sem, recv_sem):
+        return pltpu.make_async_remote_copy(
+            src_ref=src, dst_ref=dst, send_sem=send_sem, recv_sem=recv_sem,
+            device_id=plane_peer(i)[1], device_id_type=MESH,
+        )
+
+    def send_early(h):
+        def one(i, carry):
+            plane_copy(
+                i, e_send.at[h, plane_peer(i)[0]], e_recv.at[h, i], e_ss.at[h], e_rs.at[h]
+            ).start()
+            return carry
+
+        lax.fori_loop(1, nxy, one, 0)
+        e_recv[h, 0] = e_send[h, me]
+
+    e_rows = e_send.shape[2]
+    head = nxy * e_rows
+    e_send[0] = gc[0:head, 0:LANES].astype(BF).reshape(nxy, e_rows, LANES)
+    send_early(0)
+
     g_out_wide = jnp.zeros((8 * nf, 8 * c1), F32)
     for n in range(chunks):
         at = slice(n * CHUNK, (n + 1) * CHUNK)
@@ -271,36 +330,25 @@
     g_out_half = g_out_half[0:8] + g_out_half[8:16] + g_out_half[16:24] + g_out_half[24:32]
     g_out_half = g_out_half + pltpu.roll(g_out_half, 4, 0)
 
-    e_rows = e_send.shape[1]
-    full[0 : 9 * c2, :] = gc[:, 0:LANES]
     half = 9 * c2 // 2
-    full[9 * c2 : 9 * c2 + half, 0:c2] = gc[0:half, LANES : LANES + c2]
-    full[9 * c2 : 9 * c2 + half, c2 : 2 * c2] = gc[half : 2 * half, LANES : LANES + c2]
-    up_at = 9 * c2 + half
-    full[up_at : up_at + LANES, 0:c2] = gu[0:LANES]
-    full[up_at : up_at + LANES, c2 : 2 * c2] = gu[LANES : 2 * LANES]
+    tail = 9 * c2 - head
+    e_rest[0:tail, :] = gc[head:, 0:LANES].astype(BF)
+    e_rest[tail : tail + half, 0:c2] = gc[0:half, LANES : LANES + c2].astype(BF)
+    e_rest[tail : tail + half, c2 : 2 * c2] = gc[half : 2 * half, LANES : LANES + c2].astype(BF)
+    up_at = tail + half
+    e_rest[up_at : up_at + LANES, 0:c2] = gu[0:LANES].astype(BF)
+    e_rest[up_at : up_at + LANES, c2 : 2 * c2] = gu[LANES : 2 * LANES].astype(BF)
     out_at = up_at + LANES
-    full[out_at : out_at + 8, :] = g_out_half
-    full[out_at + 8 : out_at + 32, :] = jnp.zeros((24, LANES), F32)
-    e_send[...] = full[...].reshape(nxy, e_rows, LANES).astype(BF)
-
-    def plane_copy(i, src, dst, send_sem, recv_sem):
-        return pltpu.make_async_remote_copy(
-            src_ref=src, dst_ref=dst, send_sem=send_sem, recv_sem=recv_sem,
-            device_id=plane_peer(i)[1], device_id_type=MESH,
-        )
-
-    def send_early(i, carry):
-        plane_copy(i, e_send.at[plane_peer(i)[0]], e_recv.at[i], e_ss, e_rs).start()
-        return carry
-
-    lax.fori_loop(1, nxy, send_early, 0)
-    e_recv[0] = e_send[me]
-
-    finish(b_copies)
-    bc[0:c2, inner] = (b_land[0].astype(F32) * has_left).astype(BF)
-    bc[2 * c2 : 3 * c2, inner] = (b_land[1].astype(F32) * has_right).astype(BF)
+    e_rest[out_at : out_at + 32, :] = jnp.concatenate(
+        [g_out_half, jnp.zeros((24, LANES), F32)], axis=0
+    ).astype(BF)
+    e_send[1] = e_rest[...].reshape(nxy, e_rows, LANES)
+    send_early(1)
+
+    arrive(0, b_copies, b_land, bc)
     for n in range(chunks):
+        if n + 1 < chunks:
+            arrive(n + 1, b_copies, b_land, bc)
         at = slice(n * CHUNK, (n + 1) * CHUNK)
         out = sum(
             dot(wb[q], bc[:, n * CHUNK + q * LANES : (n + 1) * CHUNK + q * LANES])
@@ -323,100 +371,97 @@
         l_send[p, 0:l_rows, :] = late[p * l_rows : (p + 1) * l_rows, :]
 
     def send_late(i, carry):
-        plane_copy(i, l_send.at[plane_peer(i)[0]], l_recv.at[i], l_ss, l_rs).start()
+        plane_copy(i, l_send.at[plane_peer(i)[0], 0:l_rows], l_recv.at[i, 0:l_rows], l_ss, l_rs).start()
         return carry
 
     lax.fori_loop(1, nxy, send_late, 0)
-    l_recv[0] = l_send[me]
+    l_recv[0, 0:l_rows, :] = l_send[me, 0:l_rows, :]
+
+    def all_of(ref, sem, count, rows=None):
+        block = ref.at[pl.ds(0, count)] if rows is None else ref.at[pl.ds(0, count), 0:rows]
+        pltpu.make_async_copy(block, block, sem).wait()
+
+    def send_z(src, dst, send_sem, recv_sem):
+        def one(i, carry):
+            pltpu.make_async_remote_copy(
+                src_ref=src, dst_ref=dst, send_sem=send_sem, recv_sem=recv_sem,
+                device_id=z_peer(i)[1], device_id_type=MESH,
+            ).start()
+            return carry
+
+        lax.fori_loop(1, nzg, one, 0)
+
+    def send_plane(src, dst, send_sem, recv_sem):
+        def one(i, carry):
+            plane_copy(i, src, dst, send_sem, recv_sem).start()
+            return carry
+
+        lax.fori_loop(1, nxy, one, 0)
+
+    def early_z(h):
+        all_of(e_recv.at[h], e_rs.at[h], nxy - 1)
+        part = jnp.sum(e_recv[h].astype(F32), axis=0).astype(BF)
+        ez_out[h] = part
+        ez_all[h, zi] = part
+        send_z(ez_out.at[h], ez_all.at[h, zi], z_ss.at[h], z_rs.at[h])
+
+    def early_back(h):
+        all_of(ez_all.at[h], z_rs.at[h], nzg - 1)
+        part = jnp.sum(ez_all[h].astype(F32), axis=0).astype(BF)
+        e_out[h] = part
+        e_all[h, me] = part
+        send_plane(e_out.at[h], e_all.at[h, me], a_ss.at[h], a_rs.at[h])
+
+    early_z(0)
+    early_z(1)
 
     out = dot(dot(perm2t[...], pred_t[...]).astype(BF), join[...])
     pred[0] = out.reshape(nf, 2, ny, nz).astype(BF)
 
-    def all_of(ref, sem, count):
-        block = ref.at[pl.ds(0, count)]
-        pltpu.make_async_copy(block, block, sem).wait()
-
-    all_of(e_recv, e_rs, nxy - 1)
-    early_sum = jnp.sum(e_recv[...].astype(F32), axis=0)
-    all_of(l_recv, l_rs, nxy - 1)
-    late_sum = jnp.sum(l_recv[...], axis=0)
-
-    z_rows = -(-(e_rows + l_rows) // nzg)
-    full[0:e_rows, :] = early_sum
-    full[e_rows : e_rows + l_rows, :] = late_sum[0:l_rows]
-    for j in range(nzg):
-        z_send[j, 0:z_rows, :] = full[j * z_rows : (j + 1) * z_rows, :]
-
-    def send_z(i, carry):
-        peer, device = z_peer(i)
-        pltpu.make_async_remote_copy(
-            src_ref=z_send.at[peer], dst_ref=z_recv.at[i], send_sem=z_ss, recv_sem=z_rs,
-            device_id=device, device_id_type=MESH,
-        ).start()
-        return carry
-
-    lax.fori_loop(1, nzg, send_z, 0)
-    z_recv[0] = z_send[zi]
-    all_of(z_recv, z_rs, nzg - 1)
-    total = jnp.sum(z_recv[...], axis=0)
-    z_out[...] = total
-    z_all[zi] = total
-
-    def spread_z(i, carry):
-        pltpu.make_async_remote_copy(
-            src_ref=z_out, dst_ref=z_all.at[zi], send_sem=y_ss, recv_sem=y_rs,
-            device_id=z_peer(i)[1], device_id_type=MESH,
-        ).start()
-        return carry
-
-    lax.fori_loop(1, nzg, spread_z, 0)
-    all_of(z_all, y_rs, nzg - 1)
-    for j in range(nzg):
-        full[j * z_rows : (j + 1) * z_rows, :] = z_all[j, 0:z_rows, :]
-    e_out[...] = full[0:e_rows, :].astype(BF)
-    l_out[0:l_rows, :] = full[e_rows : e_rows + l_rows, :]
-    e_all[me] = e_out[...]
-    l_all[me] = l_out[...]
-
-    def spread_plane(i, carry):
-        plane_copy(i, e_out, e_all.at[me], a_ss, a_rs).start()
-        plane_copy(i, l_out, l_all.at[me], b_ss, b_rs).start()
-        return carry
-
-    lax.fori_loop(1, nxy, spread_plane, 0)
-
-    all_of(e_send, e_ss, nxy - 1)
-    all_of(l_send, l_ss, nxy - 1)
-    all_of(z_send, z_ss, nzg - 1)
-    all_of(z_all, y_ss, nzg - 1)
-    all_of(e_all, a_rs, nxy - 1)
-    all_of(l_all, b_rs, nxy - 1)
-    all_of(e_all, a_ss, nxy - 1)
-    all_of(l_all, b_ss, nxy - 1)
-
-    full[...] = e_all[...].astype(F32).reshape(nxy * e_rows, LANES)
-    for q in range(3):
-        for b in range(3):
-            row = (q * 3 + b) * c2
-            block = full[row : row + c2, :]
-            g_co[3 * q + b] = block[:, 0:c2]
-            g_co[9 + 3 * q + b] = pltpu.roll(block, c2, 1)[:, 0:c2]
+    all_of(l_recv, l_rs, nxy - 1, l_rows)
+    part = jnp.sum(l_recv[:, 0:l_rows, :], axis=0)
+    lz_out[0:l_rows, :] = part
+    lz_all[zi, 0:l_rows, :] = part
+    send_z(lz_out.at[0:l_rows], lz_all.at[zi, 0:l_rows], y_ss, y_rs)
+
+    early_back(0)
+    early_back(1)
+
+    all_of(lz_all, y_rs, nzg - 1, l_rows)
+    part = jnp.sum(lz_all[:, 0:l_rows, :], axis=0)
+    l_out[0:l_rows, :] = part
+    l_all[me, 0:l_rows, :] = part
+    send_plane(l_out.at[0:l_rows], l_all.at[me, 0:l_rows], b_ss, b_rs)
+
+    all_of(l_send, l_ss, nxy - 1, l_rows)
+    all_of(lz_all, y_ss, nzg - 1, l_rows)
+    for h in range(2):
+        all_of(e_send.at[h], e_ss.at[h], nxy - 1)
+        all_of(ez_all.at[h], z_ss.at[h], nzg - 1)
+        all_of(e_all.at[h], a_rs.at[h], nxy - 1)
+    full[0:head, :] = e_all[0].astype(F32).reshape(head, LANES)
+    full[head : 2 * head, :] = e_all[1].astype(F32).reshape(head, LANES)
+    for n in range(9):
+        block = full[n * c2 : (n + 1) * c2, :]
+        g_co[n] = block[:, 0:c2]
+        g_co[9 + n] = pltpu.roll(block, c2, 1)[:, 0:c2]
     for n in range(9):
         row = 9 * c2 + (n * c2) % half
         lo = min(c2, half - (n * c2) % half)
-        first, side = n * c2 // half, None
         block = full[row : row + lo, :]
-        if first == 1:
+        if n * c2 // half == 1:
             block = pltpu.roll(block, c2, 1)
         g_co[18 + n, 0:lo, :] = block[:, 0:c2]
         if lo < c2:
             rest = pltpu.roll(full[9 * c2 : 9 * c2 + c2 - lo, :], c2, 1)
             g_co[18 + n, lo:c2, :] = rest[:, 0:c2]
+    up_at, out_at = head + up_at, head + out_at
     for m in range(4):
         block = full[up_at + m * c1 : up_at + (m + 1) * c1, :]
         g_up[part_of(m)] = block[:, 0:c2]
         g_up[part_of(m + 4)] = pltpu.roll(block, c2, 1)[:, 0:c2]
     g_out[...] = full[out_at : out_at + nf, 0:c1]
+    all_of(l_all, b_rs, nxy - 1, l_rows)
     for p in range(nxy):
         late[p * l_rows : (p + 1) * l_rows, :] = l_all[p, 0:l_rows, :]
     for m in range(4):
@@ -427,6 +472,15 @@
     flipped = win_t[...].T
     for k in range(27):
         g_in[k] = flipped[k * nf : (k + 1) * nf, 0:c1]
+    for h in range(2):
+        all_of(e_all.at[h], a_ss.at[h], nxy - 1)
+    all_of(l_all, b_ss, nxy - 1, l_rows)
+
+
+def leave(*refs):
+    count = len(refs) // 2
+    for i in range(count):
+        refs[count + i][...] = refs[i][...]
 
 
 def shards(fields, cotangent, w_in, w_down, w_coarse, w_up, w_out):
@@ -435,18 +489,18 @@
     c1, c2 = w_up.shape[1], w_up.shape[2]
     cells = (ny // 2) * (nz // 2)
     nxy, nzg = ns * HIGH, nspace // HIGH
-    e_rows = (9 * c2 * 3 // 2 + LANES + 32) // nxy
+    e_rows = (9 * c2 * 3 // 2 + LANES + 32) // (2 * nxy)
     l_rows = (LANES + c1) // nxy
-    z_rows = -(-(e_rows + l_rows) // nzg)
-    zr = -(-z_rows // 4) * 4 if z_rows > 4 else 4
-    if zr > 4:
-        zr = -(-zr // 8) * 8
     lr = -(-l_rows // 8) * 8
     wide = 64 * nf
     consts = one_hots(ny, nz, nf)
     vm = pltpu.VMEM
     dma = pltpu.SemaphoreType.DMA
-    scratch = [
+    given = (
+        fields, cotangent, w_in.transpose(0, 2, 1), w_down.transpose(0, 2, 1), w_coarse, w_up,
+        w_out, *consts,
+    )
+    scratch = [vm(v.shape, v.dtype) for v in given] + [
         vm((2, nf, ny, nz), BF),
         vm((4 * nf * ny, nz), BF),
         vm(((ny + 2) * 4 * nf, 4 * LANES), BF),
@@ -480,45 +534,54 @@
         vm((c2, cells), BF),
         vm((c1, 8 * wide), BF),
         vm((9 * c2, 3 * c2), F32),
-        vm((nxy, e_rows, LANES), BF),
-        vm((nxy, e_rows, LANES), BF),
+        vm((nxy * e_rows, LANES), BF),
+        vm((2, nxy, e_rows, LANES), BF),
+        vm((2, nxy, e_rows, LANES), BF),
         vm((nxy, lr, LANES), F32),
         vm((nxy, lr, LANES), F32),
         vm((LANES + c1, LANES), F32),
-        vm((nzg, zr, LANES), F32),
-        vm((nzg, zr, LANES), F32),
-        vm((zr, LANES), F32),
-        vm((nzg, zr, LANES), F32),
-        vm((e_rows, LANES), BF),
-        vm((nxy, e_rows, LANES), BF),
+        vm((2, e_rows, LANES), BF),
+        vm((2, nzg, e_rows, LANES), BF),
+        vm((lr, LANES), F32),
+        vm((nzg, lr, LANES), F32),
+        vm((2, e_rows, LANES), BF),
+        vm((2, nxy, e_rows, LANES), BF),
         vm((lr, LANES), F32),
         vm((nxy, lr, LANES), F32),
-        vm((nxy * e_rows, LANES), F32),
-        dma((6,)), dma((6,)),
-    ] + [dma] * 12
+        vm((2 * nxy * e_rows, LANES), F32),
+        dma((13,)), dma((2 + 4 * cells // CHUNK,)), dma((2 + 4 * cells // CHUNK,)),
+        dma((2,)), dma((2,)), dma, dma, dma((2,)), dma((2,)), dma, dma, dma((2,)), dma((2,)), dma, dma,
+    ]
     shape = jax.ShapeDtypeStruct
     whole = pl.BlockSpec(memory_space=pltpu.VMEM)
+    far = pl.BlockSpec(memory_space=pltpu.HBM)
+    shapes = (
+        shape(fields.shape, BF),
+        shape((27, nf, c1), F32),
+        shape((8, c1, c2), F32),
+        shape((27, c2, c2), F32),
+        shape((8, c1, c2), F32),
+        shape((nf, c1), F32),
+    )
     outs = pl.pallas_call(
         functools.partial(body, ns, nspace),
-        out_shape=(
-            shape(fields.shape, BF),
-            shape((27, nf, c1), F32),
-            shape((8, c1, c2), F32),
-            shape((27, c2, c2), F32),
-            shape((8, c1, c2), F32),
-            shape((nf, c1), F32),
-        ),
-        in_specs=[whole] * 13,
+        out_shape=shapes,
+        in_specs=[far] * 13,
         out_specs=[whole] * 6,
         scratch_shapes=scratch,
         compiler_params=pltpu.CompilerParams(
-            collective_id=0, has_side_effects=True, vmem_limit_bytes=48 * 2**20
+            collective_id=0, has_side_effects=True, vmem_limit_bytes=VMEM
         ),
         name="unet_block",
-    )(
-        fields, cotangent, w_in.transpose(0, 2, 1), w_down.transpose(0, 2, 1), w_coarse, w_up,
-        w_out, *consts,
-    )
+    )(*given)
+    outs = pl.pallas_call(
+        leave,
+        out_shape=shapes,
+        in_specs=[whole] * 6,
+        out_specs=[whole] * 6,
+        compiler_params=pltpu.CompilerParams(vmem_limit_bytes=VMEM),
+        name="leave",
+    )(*outs)
     prediction, g_in, g_dn, g_co, g_up, g_out = outs
     return (prediction, g_in.transpose(0, 2, 1), g_dn.transpose(0, 2, 1), g_co, g_up, g_out)
 

time: 86 us -> 59.2 us (0.69)
  local copies, waits for them, and re-layouts: 15.6 us -> 0 us
  Pallas kernels: 69.1 us -> 58.4 us
    unnamed x32 -> x0, local copies, waits for them, and re-layouts: 15.6 us -> none
    pallas_call x1 -> x2, Pallas kernels: 69.1 us -> 58.4 us  [the longest x1 56 us: shards(): pl.pallas_call(functools.partial(body, ns, nspace), out_shape=shapes, in_...]
where the time goes in v2:
time: 59.2 us; the launch traced here: 59 us
  Pallas kernels  58.4 us (99%)
  between operations  0.64 us (1%)
    pallas_call x1, Pallas kernels, shards(): pl.pallas_call(functools.partial(body, ns, nspace), out_shape=shapes, in_...  56 us
    pallas_call x1, Pallas kernels, shards(): pl.pallas_call(leave, out_shape=shapes, in_specs=[whole] * 6, out_specs=[...  2.37 us

profile of v2, /device:TPU:1, one launch (start us, length us, event | category | flops | bytes accessed | tf_op | source)
XLA Modules:
  0.0 59.0 jit_solution(12922582829003585776)
XLA Ops:
  0.6 56.0 %unet_block.1 = (bf16[1,4,2,24,256]{4,3,2,1,0:T(8,128)(2,1)}, f32[27,4,32]{2,1,0:T(4,128)}, f32[8,32,64]{2,1,0:T(8,128)}, f32[27,64,64]{2,1,0:T(8,128)}, f32[8,32,64]{2,1,0:T(8,128)}, /*index=5*/f32[4,32]{1,0:T(4,128)}) custom-call(bf16[1,4,2,24,256]{4,3,2,1,0:T(8,128)(2,1)} %refs_0_.1, bf16[1,4,2,24,256]{4,3,2,1,0:T(8,128)(2,1)} %refs_1_.1, ...), custom_call_target="tpu_custom_call" | custom-call | tf_op jit(solution)/shard_map/unet_block/pallas_call | solution.py:566
  56.7 2.4 %leave.1 = (bf16[1,4,2,24,256]{4,3,2,1,0:T(8,128)(2,1)}, f32[27,4,32]{2,1,0:T(4,128)}, f32[8,32,64]{2,1,0:T(8,128)}, f32[27,64,64]{2,1,0:T(8,128)}, f32[8,32,64]{2,1,0:T(8,128)}, /*index=5*/f32[4,32]{1,0:T(4,128)}) custom-call(bf16[1,4,2,24,256]{4,3,2,1,0:T(8,128)(2,1)} %get-tuple-element.18.refs_0_, f32[27,4,32]{2,1,0:T(4,128)} %get-tuple-element.19.refs_1_, ...), custom_call_target="tpu_custom_call" | custom-call | tf_op jit(solution)/shard_map/leave/pallas_call | solution.py:577

commit v3 on v2

--- a/solution.py
+++ b/solution.py
@@ -80,7 +80,7 @@
     red_out, bc_out,
     gi_wide, gc, e_rest, e_send, e_recv, l_send, l_recv, late, ez_out, ez_all, lz_out, lz_all,
     e_out, e_all, l_out, l_all, full,
-    in_s, halo_ss, halo_rs,
+    near_p, near_z, wide_p, wide_z, in_s, halo_ss, halo_rs,
     e_ss, e_rs, l_ss, l_rs, z_ss, z_rs, y_ss, y_rs, a_ss, a_rs, b_ss, b_rs,
 ):
     fields, cot, w_in, w_dn, w_co, w_up, w_out, perm, perm2, perm2t, split, join, fold = inputs
@@ -109,20 +109,24 @@
     def greet(device):
         pl.semaphore_signal(barrier, inc=1, device_id=device, device_id_type=MESH)
 
-    def greet_plane(i, carry):
-        greet(plane_peer(i)[1])
-        return carry
-
-    def greet_far(i, carry):
-        greet(z_peer(nzg // 2 + i)[1])
-        greet(z_peer(nzg // 2 - i)[1])
-        return carry
-
-    greet(z_peer(nzg // 2)[1])
-    lax.fori_loop(1, nzg // 2, greet_far, 0)
-    lax.fori_loop(1, nxy, greet_plane, 0)
-    greet((s, left))
-    greet((s, right))
+    xs, pair = s // 4, lax.rem(s, 4)
+    mates = [xs * 4 + lax.rem(pair + i, 4) for i in (1, 2, 3)]
+    ring = [lax.rem(xs + i, ns // 4) * 4 + pair for i in range(1, ns // 4)]
+
+    def along_z(i):
+        return (s, high * nzg + lax.rem(zi + i + nzg, nzg))
+
+    opposite = (s, (1 - high) * nzg + zi)
+    greeted = [(s, left), (s, right), opposite]
+    greeted += [(mate, sp) for mate in mates] + [(other, sp) for other in ring]
+    greeted += [along_z(i) for i in (1, -1, 2, -2)]
+    for device in greeted:
+        greet(device)
+
+    def tell(sem, devices):
+        for device in devices:
+            pl.semaphore_signal(sem, inc=1, device_id=device, device_id_type=MESH)
+
     loads = [
         pltpu.make_async_copy(src, dst, in_s.at[i])
         for i, (src, dst) in enumerate(zip(given, inputs))
@@ -130,7 +134,7 @@
     for i in (0, 2, 12, 3, 5, 6, 4, 1, 8, 10, 7, 9, 11):
         loads[i].start()
     loads[0].wait()
-    pl.semaphore_wait(barrier, 2 + nxy - 1 + nzg - 1)
+    pl.semaphore_wait(barrier, len(greeted))
 
     def halo(step, to_left, to_right, from_left, from_right):
         copies = [
@@ -160,12 +164,13 @@
     hr = 2 * nf
 
     def halo_chunk(step, n, src, land):
-        at = pl.ds(n * CHUNK, CHUNK)
         return halo(
-            step * chunks + n + 1, src.at[:, at], src.at[:, at], land.at[0, :, at], land.at[1, :, at]
+            step * chunks + n + 1, src.at[n], src.at[n], land.at[0, n], land.at[1, n]
         )
 
     f_copies = halo(0, fields.at[0, :, 0], fields.at[0, :, 1], f_land.at[0], f_land.at[1])
+    tell(near_p, [(mate, sp) for mate in mates])
+    tell(near_z, [along_z(2), along_z(-2)])
     for i in (2, 12, 3, 5, 6, 4):
         loads[i].wait()
 
@@ -214,6 +219,10 @@
     rows = nf * ny
     ff[0 : 2 * rows, :] = fields[0].astype(F32).reshape(2 * rows, nz).astype(BF)
     finish(f_copies)
+    pl.semaphore_wait(near_p, 3)
+    tell(wide_p, [opposite])
+    pl.semaphore_wait(near_z, 2)
+    tell(wide_z, [along_z(4), along_z(-4)])
     ff[2 * rows : 3 * rows, :] = (f_land[0].astype(F32).reshape(rows, nz) * has_left).astype(BF)
     ff[3 * rows : 4 * rows, :] = (f_land[1].astype(F32).reshape(rows, nz) * has_right).astype(BF)
     tt[...] = dot(dot(perm[...], ff[...]).astype(BF), split[...]).astype(BF)
@@ -231,21 +240,20 @@
         fine = (pre * sigma).astype(BF)
         slope[:, at] = sigma * (1.0 + pre * (1.0 - sigma))
         act[:, at] = fine
-        red_out[:, at] = dot(wd[...], fine).astype(BF)
+        down = dot(wd[...], fine).astype(BF)
+        red_out[n] = down
+        red[c2 : 2 * c2, LANES + n * CHUNK : LANES + (n + 1) * CHUNK] = down
         r_copies.append(halo_chunk(0, n, red_out, r_land))
     edge = jnp.zeros((3 * c2, LANES), BF)
     for planes in (red, bc):
         planes[:, 0:LANES] = edge
         planes[:, LANES + cells : 2 * LANES + cells] = edge
-    inner = slice(LANES, LANES + cells)
-    red[c2 : 2 * c2, inner] = red_out[...]
 
     def arrive(n, copies, land, planes):
         finish(copies[n])
-        at = slice(n * CHUNK, (n + 1) * CHUNK)
         there = slice(LANES + n * CHUNK, LANES + (n + 1) * CHUNK)
-        planes[0:c2, there] = (land[0, :, at].astype(F32) * has_left).astype(BF)
-        planes[2 * c2 : 3 * c2, there] = (land[1, :, at].astype(F32) * has_right).astype(BF)
+        planes[0:c2, there] = (land[0, n].astype(F32) * has_left).astype(BF)
+        planes[2 * c2 : 3 * c2, there] = (land[1, n].astype(F32) * has_right).astype(BF)
 
 
     lane = lax.rem(lax.broadcasted_iota(jnp.int32, (c2, CHUNK), 1), LANES)
@@ -273,13 +281,13 @@
         sigma = jax.nn.sigmoid(pre)
         act_c[:, at] = (pre * sigma).astype(BF)
         back = (term[:, at] * (sigma * (1.0 + pre * (1.0 - sigma)))).astype(BF)
-        bc_out[:, at] = back
+        bc_out[n] = back
+        bc[c2 : 2 * c2, LANES + n * CHUNK : LANES + (n + 1) * CHUNK] = back
         b_copies.append(halo_chunk(1, n, bc_out, b_land))
         wide = back.astype(F32)
         rolled[0:c2, at] = sooner(wide).astype(BF)
         rolled[c2 : 2 * c2, at] = back
         rolled[2 * c2 : 3 * c2, at] = later(wide).astype(BF)
-    bc[c2 : 2 * c2, inner] = bc_out[...]
 
     for q in range(3):
         gc[q * 3 * c2 : (q + 1) * 3 * c2, :] = dot_nt(
@@ -303,6 +311,8 @@
 
     e_rows = e_send.shape[2]
     head = nxy * e_rows
+    pl.semaphore_wait(wide_p, 1)
+    pl.semaphore_wait(wide_z, 2)
     e_send[0] = gc[0:head, 0:LANES].astype(BF).reshape(nxy, e_rows, LANES)
     send_early(0)
 
@@ -496,6 +506,7 @@
     consts = one_hots(ny, nz, nf)
     vm = pltpu.VMEM
     dma = pltpu.SemaphoreType.DMA
+    regular = pltpu.SemaphoreType.REGULAR
     given = (
         fields, cotangent, w_in.transpose(0, 2, 1), w_down.transpose(0, 2, 1), w_coarse, w_up,
         w_out, *consts,
@@ -523,15 +534,15 @@
         vm((8 * c1, cells), BF),
         vm((c2, cells), F32),
         vm((3 * c2, cells + 2 * LANES), BF),
-        vm((2, c2, cells), BF),
+        vm((2, cells // CHUNK, c2, CHUNK), BF),
         vm((3 * c2, cells + 2 * LANES), BF),
-        vm((2, c2, cells), BF),
+        vm((2, cells // CHUNK, c2, CHUNK), BF),
         vm((3 * c2, cells), BF),
         vm((c2, cells), BF),
         vm((2 * nf * ny, 2 * LANES), BF),
         vm((8 * c1, cells), BF),
-        vm((c2, cells), BF),
-        vm((c2, cells), BF),
+        vm((cells // CHUNK, c2, CHUNK), BF),
+        vm((cells // CHUNK, c2, CHUNK), BF),
         vm((c1, 8 * wide), BF),
         vm((9 * c2, 3 * c2), F32),
         vm((nxy * e_rows, LANES), BF),
@@ -549,7 +560,7 @@
         vm((lr, LANES), F32),
         vm((nxy, lr, LANES), F32),
         vm((2 * nxy * e_rows, LANES), F32),
-        dma((13,)), dma((2 + 4 * cells // CHUNK,)), dma((2 + 4 * cells // CHUNK,)),
+        regular, regular, regular, regular, dma((13,)), dma((2 + 4 * cells // CHUNK,)), dma((2 + 4 * cells // CHUNK,)),
         dma((2,)), dma((2,)), dma, dma, dma((2,)), dma((2,)), dma, dma, dma((2,)), dma((2,)), dma, dma,
     ]
     shape = jax.ShapeDtypeStruct

time: 59.2 us -> 57.2 us (0.966)
  Pallas kernels: 58.4 us -> 56.4 us
    pallas_call x1, Pallas kernels: 56 us -> 54.1 us  [shards(): pl.pallas_call(functools.partial(body, ns, nspace), out_shape=shapes, in_...]
where the time goes in v3:
time: 57.2 us; the launch traced here: 57.1 us
  Pallas kernels  56.4 us (99%)
  between operations  0.64 us (1%)
    pallas_call x1, Pallas kernels, shards(): pl.pallas_call(functools.partial(body, ns, nspace), out_shape=shapes, in_...  54.1 us
    pallas_call x1, Pallas kernels, shards(): pl.pallas_call(leave, out_shape=shapes, in_specs=[whole] * 6, out_specs=[...  2.37 us

profile of v3, /device:TPU:1, one launch (start us, length us, event | category | flops | bytes accessed | tf_op | source)
XLA Modules:
  0.0 57.1 jit_solution(4242420317736318891)
XLA Ops:
  0.6 54.1 %unet_block.1 = (bf16[1,4,2,24,256]{4,3,2,1,0:T(8,128)(2,1)}, f32[27,4,32]{2,1,0:T(4,128)}, f32[8,32,64]{2,1,0:T(8,128)}, f32[27,64,64]{2,1,0:T(8,128)}, f32[8,32,64]{2,1,0:T(8,128)}, /*index=5*/f32[4,32]{1,0:T(4,128)}) custom-call(bf16[1,4,2,24,256]{4,3,2,1,0:T(8,128)(2,1)} %refs_0_.1, bf16[1,4,2,24,256]{4,3,2,1,0:T(8,128)(2,1)} %refs_1_.1, ...), custom_call_target="tpu_custom_call" | custom-call | tf_op jit(solution)/shard_map/unet_block/pallas_call | solution.py:577
  54.7 2.4 %leave.1 = (bf16[1,4,2,24,256]{4,3,2,1,0:T(8,128)(2,1)}, f32[27,4,32]{2,1,0:T(4,128)}, f32[8,32,64]{2,1,0:T(8,128)}, f32[27,64,64]{2,1,0:T(8,128)}, f32[8,32,64]{2,1,0:T(8,128)}, /*index=5*/f32[4,32]{1,0:T(4,128)}) custom-call(bf16[1,4,2,24,256]{4,3,2,1,0:T(8,128)(2,1)} %get-tuple-element.18.refs_0_, f32[27,4,32]{2,1,0:T(4,128)} %get-tuple-element.19.refs_1_, ...), custom_call_target="tpu_custom_call" | custom-call | tf_op jit(solution)/shard_map/leave/pallas_call | solution.py:588

commit v4 on v3

--- a/solution.py
+++ b/solution.py
@@ -69,22 +69,22 @@
     ns, nspace,
     *refs,
 ):
-    given, results, inputs, rest = refs[:13], refs[13:19], refs[19:32], refs[32:]
+    given, results, inputs, rest = refs[:13], refs[13:16], refs[16:29], refs[29:]
     work(ns, nspace, given, results, inputs, *rest)
 
 
 def work(
     ns, nspace, given, results, inputs,
     f_land, ff, tt, patches, win, win_t, wdt, wd, wu, wut, bd, bdt, wf, wb, wa,
-    act, slope, cots, cot_t, bm, term, red, r_land, bc, b_land, rolled, act_c, pred_t, bf,
+    act, slope, cots, cot_t, bm, term, red, r_land, bc, b_land, rolled, act_c, pred_t,
     red_out, bc_out,
     gi_wide, gc, e_rest, e_send, e_recv, l_send, l_recv, late, ez_out, ez_all, lz_out, lz_all,
-    e_out, e_all, l_out, l_all, full,
+    e_out, e_all, l_out, l_all,
     near_p, near_z, wide_p, wide_z, in_s, halo_ss, halo_rs,
     e_ss, e_rs, l_ss, l_rs, z_ss, z_rs, y_ss, y_rs, a_ss, a_rs, b_ss, b_rs,
 ):
     fields, cot, w_in, w_dn, w_co, w_up, w_out, perm, perm2, perm2t, split, join, fold = inputs
-    pred, g_in, g_dn, g_co, g_up, g_out = results
+    pred, got_e, got_l = results
     nzg = nspace // HIGH
     nxy = ns * HIGH
     s = lax.axis_index("sample")
@@ -356,6 +356,8 @@
     send_early(1)
 
     arrive(0, b_copies, b_land, bc)
+    gd = jnp.zeros((8 * c1, c2), F32)
+    gi = jnp.zeros((8 * c1, 64 * nf), F32)
     for n in range(chunks):
         if n + 1 < chunks:
             arrive(n + 1, b_copies, b_land, bc)
@@ -366,13 +368,12 @@
         )
         back = out[c2 : 2 * c2] + sooner(out[0:c2]) + later(out[2 * c2 : 3 * c2])
         back = back.astype(BF)
-        bc_out_at = rolled
-        bc_out_at[0:c2, at] = back
-        bf[:, at] = ((bm[:, at].astype(F32) + dot(wdt[...], back)) * slope[:, at]).astype(BF)
-    gd = dot_nt(act[...], rolled[0:c2, :])
+        fine = ((bm[:, at].astype(F32) + dot(wdt[...], back)) * slope[:, at]).astype(BF)
+        gd = gd + dot_nt(act[:, at], back)
+        gi = gi + dot_nt(fine, patches[:, at])
     late[0:LANES, 0:c2] = gd[0:LANES]
     late[0:LANES, c2 : 2 * c2] = gd[LANES : 2 * LANES]
-    gi = dot_nt(bf[...], patches[...]).astype(BF)
+    gi = gi.astype(BF)
     for m in range(8):
         gi_wide[:, m * 64 * nf : (m + 1) * 64 * nf] = gi[m * c1 : (m + 1) * c1, :]
     late[LANES : LANES + c1, :] = dot_nt(gi_wide[...], fold[...])
@@ -392,14 +393,19 @@
         pltpu.make_async_copy(block, block, sem).wait()
 
     def send_z(src, dst, send_sem, recv_sem):
-        def one(i, carry):
+        def one(i):
             pltpu.make_async_remote_copy(
                 src_ref=src, dst_ref=dst, send_sem=send_sem, recv_sem=recv_sem,
                 device_id=z_peer(i)[1], device_id_type=MESH,
             ).start()
+
+        def both(i, carry):
+            one(nzg // 2 + i)
+            one(nzg // 2 - i)
             return carry
 
-        lax.fori_loop(1, nzg, one, 0)
+        one(nzg // 2)
+        lax.fori_loop(1, nzg // 2, both, 0)
 
     def send_plane(src, dst, send_sem, recv_sem):
         def one(i, carry):
@@ -449,8 +455,26 @@
         all_of(e_send.at[h], e_ss.at[h], nxy - 1)
         all_of(ez_all.at[h], z_ss.at[h], nzg - 1)
         all_of(e_all.at[h], a_rs.at[h], nxy - 1)
-    full[0:head, :] = e_all[0].astype(F32).reshape(head, LANES)
-    full[head : 2 * head, :] = e_all[1].astype(F32).reshape(head, LANES)
+    got_e[...] = e_all[...]
+    all_of(l_all, b_rs, nxy - 1, l_rows)
+    got_l[...] = l_all[...]
+    for h in range(2):
+        all_of(e_all.at[h], a_ss.at[h], nxy - 1)
+    all_of(l_all, b_ss, nxy - 1, l_rows)
+
+
+def leave(
+    prediction, got_e, got_l, pred, g_in, g_dn, g_co, g_up, g_out, full, late, win_t
+):
+    nf, c1 = g_out.shape
+    c2 = g_co.shape[1]
+    nxy, e_rows = got_e.shape[1], got_e.shape[2]
+    l_rows = (LANES + c1) // nxy
+    head, half = nxy * e_rows, 9 * c2 // 2
+    pred[...] = prediction[...]
+    win_t[...] = jnp.zeros_like(win_t)
+    full[0:head, :] = got_e[0].astype(F32).reshape(head, LANES)
+    full[head : 2 * head, :] = got_e[1].astype(F32).reshape(head, LANES)
     for n in range(9):
         block = full[n * c2 : (n + 1) * c2, :]
         g_co[n] = block[:, 0:c2]
@@ -465,15 +489,15 @@
         if lo < c2:
             rest = pltpu.roll(full[9 * c2 : 9 * c2 + c2 - lo, :], c2, 1)
             g_co[18 + n, lo:c2, :] = rest[:, 0:c2]
-    up_at, out_at = head + up_at, head + out_at
+    up_at = 9 * c2 + half
+    out_at = up_at + LANES
     for m in range(4):
         block = full[up_at + m * c1 : up_at + (m + 1) * c1, :]
         g_up[part_of(m)] = block[:, 0:c2]
         g_up[part_of(m + 4)] = pltpu.roll(block, c2, 1)[:, 0:c2]
     g_out[...] = full[out_at : out_at + nf, 0:c1]
-    all_of(l_all, b_rs, nxy - 1, l_rows)
     for p in range(nxy):
-        late[p * l_rows : (p + 1) * l_rows, :] = l_all[p, 0:l_rows, :]
+        late[p * l_rows : (p + 1) * l_rows, :] = got_l[p, 0:l_rows, :]
     for m in range(4):
         block = late[m * c1 : (m + 1) * c1, :]
         g_dn[part_of(m)] = block[:, 0:c2]
@@ -482,15 +506,6 @@
     flipped = win_t[...].T
     for k in range(27):
         g_in[k] = flipped[k * nf : (k + 1) * nf, 0:c1]
-    for h in range(2):
-        all_of(e_all.at[h], a_ss.at[h], nxy - 1)
-    all_of(l_all, b_ss, nxy - 1, l_rows)
-
-
-def leave(*refs):
-    count = len(refs) // 2
-    for i in range(count):
-        refs[count + i][...] = refs[i][...]
 
 
 def shards(fields, cotangent, w_in, w_down, w_coarse, w_up, w_out):
@@ -540,7 +555,6 @@
         vm((3 * c2, cells), BF),
         vm((c2, cells), BF),
         vm((2 * nf * ny, 2 * LANES), BF),
-        vm((8 * c1, cells), BF),
         vm((cells // CHUNK, c2, CHUNK), BF),
         vm((cells // CHUNK, c2, CHUNK), BF),
         vm((c1, 8 * wide), BF),
@@ -559,7 +573,6 @@
         vm((2, nxy, e_rows, LANES), BF),
         vm((lr, LANES), F32),
         vm((nxy, lr, LANES), F32),
-        vm((2 * nxy * e_rows, LANES), F32),
         regular, regular, regular, regular, dma((13,)), dma((2 + 4 * cells // CHUNK,)), dma((2 + 4 * cells // CHUNK,)),
         dma((2,)), dma((2,)), dma, dma, dma((2,)), dma((2,)), dma, dma, dma((2,)), dma((2,)), dma, dma,
     ]
@@ -576,9 +589,11 @@
     )
     outs = pl.pallas_call(
         functools.partial(body, ns, nspace),
-        out_shape=shapes,
+        out_shape=(
+            shapes[0], shape((2, nxy, e_rows, LANES), BF), shape((nxy, lr, LANES), F32),
+        ),
         in_specs=[far] * 13,
-        out_specs=[whole] * 6,
+        out_specs=[whole] * 3,
         scratch_shapes=scratch,
         compiler_params=pltpu.CompilerParams(
             collective_id=0, has_side_effects=True, vmem_limit_bytes=VMEM
@@ -588,8 +603,11 @@
     outs = pl.pallas_call(
         leave,
         out_shape=shapes,
-        in_specs=[whole] * 6,
+        in_specs=[whole] * 3,
         out_specs=[whole] * 6,
+        scratch_shapes=[
+            vm((2 * nxy * e_rows, LANES), F32), vm((LANES + c1, LANES), F32), vm((128, 128), F32),
+        ],
         compiler_params=pltpu.CompilerParams(vmem_limit_bytes=VMEM),
         name="leave",
     )(*outs)

time: 57.2 us -> 55.9 us (0.977)
  Pallas kernels: 56.4 us -> 55.1 us
    pallas_call x2, Pallas kernels: 56.4 us -> 55.1 us  [the longest x1 52.9 us: shards(): pl.pallas_call(functools.partial(body, ns, nspace), out_shape=(shapes[0],...]
where the time goes in v4:
time: 55.9 us; the launch traced here: 55.8 us
  Pallas kernels  55.1 us (99%)
  between operations  0.64 us (1%)
    pallas_call x1, Pallas kernels, shards(): pl.pallas_call(functools.partial(body, ns, nspace), out_shape=(shapes[0],...  52.9 us
    pallas_call x1, Pallas kernels, shards(): pl.pallas_call(leave, out_shape=shapes, in_specs=[whole] * 3, out_specs=[...  2.28 us

profile of v4, /device:TPU:1, one launch (start us, length us, event | category | flops | bytes accessed | tf_op | source)
XLA Modules:
  0.0 55.8 jit_solution(16015188003516849124)
XLA Ops:
  0.6 52.9 %unet_block.1 = (bf16[1,4,2,24,256]{4,3,2,1,0:T(8,128)(2,1)}, bf16[2,32,16,128]{3,2,1,0:T(8,128)(2,1)}, f32[32,8,128]{2,1,0:T(8,128)}) custom-call(bf16[1,4,2,24,256]{4,3,2,1,0:T(8,128)(2,1)} %refs_0_.1, bf16[1,4,2,24,256]{4,3,2,1,0:T(8,128)(2,1)} %refs_1_.1, bf16[27,4,32]{2,1,0:T(4,128)(2,1)} %bitcast.5, bf16[8,32,64]{2,1,0:T(8,128)(2,1)} %bitcast.4, ...), custom_call_target="tpu_custom_call" | custom-call | tf_op jit(solution)/shard_map/unet_block/pallas_call | solution.py:590
  53.5 2.3 %leave.1 = (bf16[1,4,2,24,256]{4,3,2,1,0:T(8,128)(2,1)}, f32[27,4,32]{2,1,0:T(4,128)}, f32[8,32,64]{2,1,0:T(8,128)}, f32[27,64,64]{2,1,0:T(8,128)}, f32[8,32,64]{2,1,0:T(8,128)}, /*index=5*/f32[4,32]{1,0:T(4,128)}) custom-call(bf16[1,4,2,24,256]{4,3,2,1,0:T(8,128)(2,1)} %get-tuple-element.15.prediction, bf16[2,32,16,128]{3,2,1,0:T(8,128)(2,1)} %get-tuple-element.16.got_e, ...), custom_call_target="tpu_custom_call" | custom-call | tf_op jit(solution)/shard_map/leave/pallas_call | solution.py:603

commit v5 on v4

--- a/solution.py
+++ b/solution.py
@@ -12,7 +12,7 @@
 BF = jnp.bfloat16
 F32 = jnp.float32
 LANES = 128
-CHUNK = 256
+CHUNK = 512
 VMEM = 63 * 2**20
 HIGH = 2
 

time: 55.9 us -> 53.8 us (0.962)
  Pallas kernels: 55.1 us -> 53 us
    pallas_call x1, Pallas kernels: 52.9 us -> 50.7 us  [shards(): pl.pallas_call(functools.partial(body, ns, nspace), out_shape=(shapes[0],...]
where the time goes in v5:
time: 53.8 us; the launch traced here: 53.6 us
  Pallas kernels  53 us (99%)
  between operations  0.64 us (1%)
    pallas_call x1, Pallas kernels, shards(): pl.pallas_call(functools.partial(body, ns, nspace), out_shape=(shapes[0],...  50.7 us
    pallas_call x1, Pallas kernels, shards(): pl.pallas_call(leave, out_shape=shapes, in_specs=[whole] * 3, out_specs=[...  2.28 us

profile of v5, /device:TPU:1, one launch (start us, length us, event | category | flops | bytes accessed | tf_op | source)
XLA Modules:
  0.0 53.6 jit_solution(4606112749606025290)
XLA Ops:
  0.6 50.7 %unet_block.1 = (bf16[1,4,2,24,256]{4,3,2,1,0:T(8,128)(2,1)}, bf16[2,32,16,128]{3,2,1,0:T(8,128)(2,1)}, f32[32,8,128]{2,1,0:T(8,128)}) custom-call(bf16[1,4,2,24,256]{4,3,2,1,0:T(8,128)(2,1)} %refs_0_.1, bf16[1,4,2,24,256]{4,3,2,1,0:T(8,128)(2,1)} %refs_1_.1, bf16[27,4,32]{2,1,0:T(4,128)(2,1)} %bitcast.5, bf16[8,32,64]{2,1,0:T(8,128)(2,1)} %bitcast.4, ...), custom_call_target="tpu_custom_call" | custom-call | tf_op jit(solution)/shard_map/unet_block/pallas_call | solution.py:590
  51.4 2.3 %leave.1 = (bf16[1,4,2,24,256]{4,3,2,1,0:T(8,128)(2,1)}, f32[27,4,32]{2,1,0:T(4,128)}, f32[8,32,64]{2,1,0:T(8,128)}, f32[27,64,64]{2,1,0:T(8,128)}, f32[8,32,64]{2,1,0:T(8,128)}, /*index=5*/f32[4,32]{1,0:T(4,128)}) custom-call(bf16[1,4,2,24,256]{4,3,2,1,0:T(8,128)(2,1)} %get-tuple-element.15.prediction, bf16[2,32,16,128]{3,2,1,0:T(8,128)(2,1)} %get-tuple-element.16.got_e, ...), custom_call_target="tpu_custom_call" | custom-call | tf_op jit(solution)/shard_map/leave/pallas_call | solution.py:603

commit v6 on v5

--- a/solution.py
+++ b/solution.py
@@ -163,9 +163,14 @@
     fr = 4 * nf
     hr = 2 * nf
 
-    def halo_chunk(step, n, src, land):
+    ends_b = [n * CHUNK for n in range(chunks)] + [cells]
+    ends_c = [0] + [n * CHUNK + LANES for n in range(1, chunks)] + [cells]
+    ends_f = [0] + [n * CHUNK + 2 * LANES for n in range(1, chunks)] + [cells]
+
+    def halo_chunk(step, n, src, land, ends):
+        at = pl.ds(ends[n], ends[n + 1] - ends[n])
         return halo(
-            step * chunks + n + 1, src.at[n], src.at[n], land.at[0, n], land.at[1, n]
+            step * chunks + n + 1, src.at[:, at], src.at[:, at], land.at[0, :, at], land.at[1, :, at]
         )
 
     f_copies = halo(0, fields.at[0, :, 0], fields.at[0, :, 1], f_land.at[0], f_land.at[1])
@@ -234,56 +239,56 @@
                 ]
     r_copies = []
     for n in range(chunks):
-        at = slice(n * CHUNK, (n + 1) * CHUNK)
+        at = slice(ends_f[n], ends_f[n + 1])
         pre = dot(win[...], patches[:, at])
         sigma = jax.nn.sigmoid(pre)
         fine = (pre * sigma).astype(BF)
         slope[:, at] = sigma * (1.0 + pre * (1.0 - sigma))
         act[:, at] = fine
         down = dot(wd[...], fine).astype(BF)
-        red_out[n] = down
-        red[c2 : 2 * c2, LANES + n * CHUNK : LANES + (n + 1) * CHUNK] = down
-        r_copies.append(halo_chunk(0, n, red_out, r_land))
+        red_out[:, at] = down
+        red[c2 : 2 * c2, LANES + ends_f[n] : LANES + ends_f[n + 1]] = down
+        r_copies.append(halo_chunk(0, n, red_out, r_land, ends_f))
     edge = jnp.zeros((3 * c2, LANES), BF)
     for planes in (red, bc):
         planes[:, 0:LANES] = edge
         planes[:, LANES + cells : 2 * LANES + cells] = edge
 
-    def arrive(n, copies, land, planes):
+    def arrive(n, copies, land, planes, ends):
         finish(copies[n])
-        there = slice(LANES + n * CHUNK, LANES + (n + 1) * CHUNK)
-        planes[0:c2, there] = (land[0, n].astype(F32) * has_left).astype(BF)
-        planes[2 * c2 : 3 * c2, there] = (land[1, n].astype(F32) * has_right).astype(BF)
-
-
-    lane = lax.rem(lax.broadcasted_iota(jnp.int32, (c2, CHUNK), 1), LANES)
-    not_first, not_last = lane > 0, lane < LANES - 1
+        at = slice(ends[n], ends[n + 1])
+        there = slice(LANES + ends[n], LANES + ends[n + 1])
+        planes[0:c2, there] = (land[0, :, at].astype(F32) * has_left).astype(BF)
+        planes[2 * c2 : 3 * c2, there] = (land[1, :, at].astype(F32) * has_right).astype(BF)
+
+
+    def lane_of(v):
+        return lax.rem(lax.broadcasted_iota(jnp.int32, v.shape, 1), LANES)
 
     def later(v):
-        return jnp.where(not_first, pltpu.roll(v, 1, 1), 0.0)
+        return jnp.where(lane_of(v) > 0, pltpu.roll(v, 1, 1), 0.0)
 
     def sooner(v):
-        return jnp.where(not_last, pltpu.roll(v, CHUNK - 1, 1), 0.0)
+        return jnp.where(lane_of(v) < LANES - 1, pltpu.roll(v, v.shape[1] - 1, 1), 0.0)
 
     wf_b = [wf[q].astype(BF) for q in range(3)]
 
     b_copies = []
-    arrive(0, r_copies, r_land, red)
     for n in range(chunks):
-        if n + 1 < chunks:
-            arrive(n + 1, r_copies, r_land, red)
-        at = slice(n * CHUNK, (n + 1) * CHUNK)
+        arrive(n, r_copies, r_land, red, ends_f)
+        lo, hi = ends_c[n], ends_c[n + 1]
+        at = slice(lo, hi)
         out = sum(
-            dot(wf_b[q], red[:, n * CHUNK + q * LANES : (n + 1) * CHUNK + q * LANES])
+            dot(wf_b[q], red[:, lo + q * LANES : hi + q * LANES])
             for q in range(3)
         )
         pre = out[c2 : 2 * c2] + later(out[0:c2]) + sooner(out[2 * c2 : 3 * c2])
         sigma = jax.nn.sigmoid(pre)
         act_c[:, at] = (pre * sigma).astype(BF)
         back = (term[:, at] * (sigma * (1.0 + pre * (1.0 - sigma)))).astype(BF)
-        bc_out[n] = back
-        bc[c2 : 2 * c2, LANES + n * CHUNK : LANES + (n + 1) * CHUNK] = back
-        b_copies.append(halo_chunk(1, n, bc_out, b_land))
+        bc_out[:, at] = back
+        bc[c2 : 2 * c2, LANES + lo : LANES + hi] = back
+        b_copies.append(halo_chunk(1, n, bc_out, b_land, ends_c))
         wide = back.astype(F32)
         rolled[0:c2, at] = sooner(wide).astype(BF)
         rolled[c2 : 2 * c2, at] = back
@@ -355,12 +360,10 @@
     e_send[1] = e_rest[...].reshape(nxy, e_rows, LANES)
     send_early(1)
 
-    arrive(0, b_copies, b_land, bc)
     gd = jnp.zeros((8 * c1, c2), F32)
     gi = jnp.zeros((8 * c1, 64 * nf), F32)
     for n in range(chunks):
-        if n + 1 < chunks:
-            arrive(n + 1, b_copies, b_land, bc)
+        arrive(n, b_copies, b_land, bc, ends_c)
         at = slice(n * CHUNK, (n + 1) * CHUNK)
         out = sum(
             dot(wb[q], bc[:, n * CHUNK + q * LANES : (n + 1) * CHUNK + q * LANES])
@@ -549,14 +552,14 @@
         vm((8 * c1, cells), BF),
         vm((c2, cells), F32),
         vm((3 * c2, cells + 2 * LANES), BF),
-        vm((2, cells // CHUNK, c2, CHUNK), BF),
+        vm((2, c2, cells), BF),
         vm((3 * c2, cells + 2 * LANES), BF),
-        vm((2, cells // CHUNK, c2, CHUNK), BF),
+        vm((2, c2, cells), BF),
         vm((3 * c2, cells), BF),
         vm((c2, cells), BF),
         vm((2 * nf * ny, 2 * LANES), BF),
-        vm((cells // CHUNK, c2, CHUNK), BF),
-        vm((cells // CHUNK, c2, CHUNK), BF),
+        vm((c2, cells), BF),
+        vm((c2, cells), BF),
         vm((c1, 8 * wide), BF),
         vm((9 * c2, 3 * c2), F32),
         vm((nxy * e_rows, LANES), BF),

time: 53.8 us -> 54 us (level)
  no operation moved by 1% of the time
where the time goes in v6:
time: 54 us; the launch traced here: 53.9 us
  Pallas kernels  53.2 us (99%)
  between operations  0.64 us (1%)
    pallas_call x1, Pallas kernels, shards(): pl.pallas_call(functools.partial(body, ns, nspace), out_shape=(shapes[0],...  50.9 us
    pallas_call x1, Pallas kernels, shards(): pl.pallas_call(leave, out_shape=shapes, in_specs=[whole] * 3, out_specs=[...  2.28 us

profile of v6, /device:TPU:1, one launch (start us, length us, event | category | flops | bytes accessed | tf_op | source)
XLA Modules:
  0.0 53.9 jit_solution(14535265574756878595)
XLA Ops:
  0.6 50.9 %unet_block.1 = (bf16[1,4,2,24,256]{4,3,2,1,0:T(8,128)(2,1)}, bf16[2,32,16,128]{3,2,1,0:T(8,128)(2,1)}, f32[32,8,128]{2,1,0:T(8,128)}) custom-call(bf16[1,4,2,24,256]{4,3,2,1,0:T(8,128)(2,1)} %refs_0_.1, bf16[1,4,2,24,256]{4,3,2,1,0:T(8,128)(2,1)} %refs_1_.1, bf16[27,4,32]{2,1,0:T(4,128)(2,1)} %bitcast.5, bf16[8,32,64]{2,1,0:T(8,128)(2,1)} %bitcast.4, ...), custom_call_target="tpu_custom_call" | custom-call | tf_op jit(solution)/shard_map/unet_block/pallas_call | solution.py:593
  51.6 2.3 %leave.1 = (bf16[1,4,2,24,256]{4,3,2,1,0:T(8,128)(2,1)}, f32[27,4,32]{2,1,0:T(4,128)}, f32[8,32,64]{2,1,0:T(8,128)}, f32[27,64,64]{2,1,0:T(8,128)}, f32[8,32,64]{2,1,0:T(8,128)}, /*index=5*/f32[4,32]{1,0:T(4,128)}) custom-call(bf16[1,4,2,24,256]{4,3,2,1,0:T(8,128)(2,1)} %get-tuple-element.15.prediction, bf16[2,32,16,128]{3,2,1,0:T(8,128)(2,1)} %get-tuple-element.16.got_e, ...), custom_call_target="tpu_custom_call" | custom-call | tf_op jit(solution)/shard_map/leave/pallas_call | solution.py:606
